TPU v7x, 256 devices: a whole 4x4x8 slice. The times are simulated.
256 devices in a mesh: dp: 2 (over core), ctx: 128 (over y, x, z).
Axes of the slice: x: 4, y: 4, z: 8, core: 2. Of those that a mesh axis runs over, the one named last changes fastest.
Arguments:
- features: bfloat16 [2, 32768, 2560], P('dp', 'ctx'), may hold values from -6 to 6
- write_keys: bfloat16 [2, 32768, 128], P('dp', 'ctx'), may hold values from -0.75 to 0.75
- read_queries: bfloat16 [2, 32768, 128], P('dp', 'ctx'), may hold values from -0.75 to 0.75
- step_logits: float32 [2, 40, 32768], P('dp', None, 'ctx'), may hold values from -6 to 6
- step_bias: float32 [40], replicated, may hold values from -1 to 1
- decay_log: float32 [40], replicated, may hold values from -16 to -2
- skip_gain: float32 [40], replicated, may hold values from 0.5 to 1.5
- doc_starts: int32 [2, 32], P('dp'), may hold values from 0 to 32767, as said below
- out_grad: bfloat16 [2, 32768, 2560], P('dp', 'ctx'), may hold values from -20 to 20
Outputs:
- mixed: bfloat16 [2, 32768, 2560], P('dp', 'ctx')
- feature_grad: bfloat16 [2, 32768, 2560], P('dp', 'ctx')
- write_grad: bfloat16 [2, 32768, 128], P('dp', 'ctx')
- read_grad: bfloat16 [2, 32768, 128], P('dp', 'ctx')
- step_grad: float32 [2, 40, 32768], P('dp', None, 'ctx')
- bias_grad: float32 [40], replicated
- decay_grad: float32 [40], replicated
- skip_grad: float32 [40], replicated
Inputs may be any that keep to these rules, and one draw needn't show every extreme that they name: `doc_starts`: each row is ascending with distinct entries, begins with 0 and ends with 32767; row b holds the first positions of the documents packed into sequence b.
All inputs are finite; a program needn't handle non-finite values.
Results may differ from a plain program's by a relative error of at most 0.002.
Values sent between devices are 32-bit elements; how exact they have to be, the bound alone decides.
A program may use at most 128 MiB of HBM per device.

v0:
```python
import jax
import jax.numpy as jnp
from jax import lax
from jax.sharding import PartitionSpec as P

GROUP_HEADS = 2


EXACT = lax.Precision.HIGHEST


def swapped(value, axis, distance):
    mask = 2**distance
    pairs = [(source, source ^ mask) for source in range(lax.axis_size(axis))]
    return lax.ppermute(value, axis, pairs)


def widen(values, repeat_by):
    return jnp.repeat(values, repeat_by, axis=-1)


def step_decays(logit_block, step_bias, decay_log):
    stride = jax.nn.softplus(logit_block + step_bias[:, None])
    decay_rate = -jnp.exp(decay_log)
    cumulative = jnp.cumsum(stride * decay_rate[:, None], axis=1)
    return (stride, cumulative)


def segments(doc_starts, start_pos, length):
    positions = start_pos + jnp.arange(length, dtype=jnp.int32)
    segment = jnp.sum((doc_starts[None, :] <= positions[:, None]).astype(jnp.int32), axis=1)
    entry_segment = jnp.sum((doc_starts <= start_pos - 1).astype(jnp.int32))
    return (segment, entry_segment)


def block_state(feature_block, write_block, logit_block, step_bias, decay_log, own_last, linked):
    stride, cumulative = step_decays(logit_block, step_bias, decay_log)
    weights = own_last[None, :] * jnp.exp(cumulative[:, -1:] - cumulative) * stride
    head_size = feature_block.shape[1] // stride.shape[0]
    scaled = feature_block * widen(weights.T, head_size)
    state_end = jnp.dot(write_block.T, scaled, precision=EXACT, preferred_element_type=jnp.float32)
    totals = jnp.exp(cumulative[:, -1]) * linked
    return (state_end, totals)


def intra_group(cum_group, stride_group, feature_group, scores, same_doc):
    gaps = cum_group[:, :, None] - cum_group[:, None, :]
    decays = jnp.exp(jnp.where(same_doc[None], gaps, -jnp.inf))
    mixing = decays * scores[None] * stride_group[:, None, :]
    head_count = cum_group.shape[0]
    per_head = feature_group.reshape(feature_group.shape[0], head_count, -1)
    result = jnp.einsum("htu,uhp->thp", mixing, per_head, precision=EXACT)
    return result.reshape(feature_group.shape[0], -1)


def block_main(
    feature_block, write_block, read_block, logit_block, step_bias, decay_log, skip_gain, segment
):
    stride, cumulative = step_decays(logit_block, step_bias, decay_log)
    length = feature_block.shape[0]
    head_count = stride.shape[0]
    head_size = feature_block.shape[1] // head_count
    groups = head_count // GROUP_HEADS
    ordinal = jnp.arange(length, dtype=jnp.int32)
    same_doc = (segment[:, None] == segment[None, :]) & (ordinal[:, None] >= ordinal[None, :])
    scores = jnp.dot(read_block, write_block.T, precision=EXACT, preferred_element_type=jnp.float32)
    cum_stack = cumulative.reshape(groups, GROUP_HEADS, length)
    stride_stack = stride.reshape(groups, GROUP_HEADS, length)
    feature_stack = feature_block.reshape(length, groups, GROUP_HEADS * head_size).transpose(
        1, 0, 2
    )

    def one_group(packed):
        return intra_group(packed[0], packed[1], packed[2], scores, same_doc)

    pieces = lax.map(jax.checkpoint(one_group), (cum_stack, stride_stack, feature_stack))
    inside = pieces.transpose(1, 0, 2).reshape(length, -1)
    return inside + feature_block * widen(skip_gain, head_size)


def block_carry(read_block, logit_block, step_bias, decay_log, keep_in, state_in):
    stride, cumulative = step_decays(logit_block, step_bias, decay_log)
    factor = keep_in[:, None] * jnp.exp(cumulative.T)
    head_size = state_in.shape[1] // factor.shape[1]
    return jnp.dot(
        read_block, state_in, precision=EXACT, preferred_element_type=jnp.float32
    ) * widen(factor, head_size)


def link_states(earlier, latter):
    head_size = latter[1].shape[1] // latter[0].shape[0]
    return (earlier[0] * latter[0], earlier[1] * widen(latter[0], head_size)[None, :] + latter[1])


def select_pair(condition, first, second):
    return jax.tree.map(lambda left, right: jnp.where(condition, left, right), first, second)


def local(
    features,
    write_keys,
    read_queries,
    step_logits,
    step_bias,
    decay_log,
    skip_gain,
    doc_starts,
    out_grad,
):
    length = features.shape[1]
    position = lax.axis_index("ctx")
    bit_count = lax.axis_size("ctx").bit_length() - 1
    start_pos = position * length
    segment, entry_segment = segments(doc_starts[0], start_pos, length)
    keep_in = (segment == entry_segment).astype(jnp.float32)
    own_last = (segment == segment[-1]).astype(jnp.float32)
    linked = (segment[-1] == entry_segment).astype(jnp.float32)
    feature_full = features[0].astype(jnp.float32)
    write_full = write_keys[0].astype(jnp.float32)
    read_full = read_queries[0].astype(jnp.float32)
    logit_full = step_logits[0]

    def state_fn(feat_in, write_in, logit_in, bias_in, decay_in):
        return block_state(feat_in, write_in, logit_in, bias_in, decay_in, own_last, linked)

    (state_end, totals), state_back = jax.vjp(
        state_fn, feature_full, write_full, logit_full, step_bias, decay_log
    )
    head_count = totals.shape[0]

    def main_fn(feat_in, write_in, read_in, logit_in, bias_in, decay_in, skip_in):
        return block_main(feat_in, write_in, read_in, logit_in, bias_in, decay_in, skip_in, segment)

    def carry_fn(read_in, logit_in, bias_in, decay_in, state_arg):
        return block_carry(read_in, logit_in, bias_in, decay_in, keep_in, state_arg)

    identity = (jnp.ones_like(totals), jnp.zeros_like(state_end))
    forward_prefix = identity
    forward_total = (totals, state_end)
    for bit in range(bit_count):
        other = swapped((forward_total[0], forward_total[1]), "ctx", bit)
        partner_first = position >> bit & 1 == 1
        forward_prefix = select_pair(
            partner_first, link_states(other, forward_prefix), forward_prefix
        )
        forward_total = select_pair(
            partner_first, link_states(other, forward_total), link_states(forward_total, other)
        )
    state_in = forward_prefix[1]
    cotangent = out_grad[0].astype(jnp.float32)

    def whole_fn(feat_in, write_in, read_in, logit_in, bias_in, decay_in, skip_in, state_arg):
        return main_fn(feat_in, write_in, read_in, logit_in, bias_in, decay_in, skip_in) + carry_fn(
            read_in, logit_in, bias_in, decay_in, state_arg
        )

    mixed_out, whole_back = jax.vjp(
        whole_fn,
        feature_full,
        write_full,
        read_full,
        logit_full,
        step_bias,
        decay_log,
        skip_gain,
        state_in,
    )
    feat_main, write_main, read_main, logit_main, bias_main, decay_main, skip_total, state_grad = (
        whole_back(cotangent)
    )
    backward_prefix = identity
    backward_total = (totals, state_grad)
    for bit in range(bit_count):
        other = swapped((backward_total[0], backward_total[1]), "ctx", bit)
        partner_first = position >> bit & 1 == 0
        backward_prefix = select_pair(
            partner_first, link_states(other, backward_prefix), backward_prefix
        )
        backward_total = select_pair(
            partner_first, link_states(other, backward_total), link_states(backward_total, other)
        )
    adjoint = backward_prefix[1]
    total_grad = jnp.sum(
        (adjoint * state_in).reshape(adjoint.shape[0], head_count, -1), axis=(0, 2)
    )
    feat_state, write_state, logit_state, bias_state, decay_state = state_back(
        (adjoint, total_grad)
    )
    bias_sum, decay_sum, skip_sum = lax.psum(
        (bias_main + bias_state, decay_main + decay_state, skip_total), ("dp", "ctx")
    )
    return (
        mixed_out.astype(jnp.bfloat16)[None],
        (feat_main + feat_state).astype(jnp.bfloat16)[None],
        (write_main + write_state).astype(jnp.bfloat16)[None],
        read_main.astype(jnp.bfloat16)[None],
        (logit_main + logit_state)[None],
        bias_sum,
        decay_sum,
        skip_sum,
    )


def solution(mesh):
    in_specs = (
        P("dp", "ctx", None),
        P("dp", "ctx", None),
        P("dp", "ctx", None),
        P("dp", None, "ctx"),
        P(),
        P(),
        P(),
        P("dp", None),
        P("dp", "ctx", None),
    )
    out_specs = (
        P("dp", "ctx", None),
        P("dp", "ctx", None),
        P("dp", "ctx", None),
        P("dp", "ctx", None),
        P("dp", None, "ctx"),
        P(),
        P(),
        P(),
    )
    return jax.shard_map(local, mesh=mesh, in_specs=in_specs, out_specs=out_specs, check_vma=False)
```

profile of v0, /device:TPU:1, one launch (start us, length us, event | category | flops | bytes accessed | tf_op | source)
XLA Modules:
  0.0 832.4 jit_solution(5739153854110955840)
XLA Ops:
  8.0 2.0 compare_convert_fusion.2
  14.1 2.4 convolution_bitcast_fusion.3
  16.5 2.5 collective-permute-start
  19.0 2.4 copy.112
  24.5 2.4 convolution_bitcast_fusion.2
  29.9 44.9 %collective-permute-done.1 = f32[40]{0:T(128)S(1)} collective-permute-done((f32[40]{0:T(128)S(1)}, f32[40]{0:T(128)S(1)}, u32[]{:S(2)}, u32[]{:S(2)}) %collective-permute-start.1) | collective-permute-done | bytes 192 | tf_op jit(solution)/shard_map/ppermute | solution.py:15
  74.9 4.2 add_select_fusion.23
  79.2 3.9 collective-permute-start.14
  83.2 2.4 collective-permute-start.3
  85.7 110.2 %collective-permute-done.3 = f32[40]{0:T(128)S(1)} collective-permute-done((f32[40]{0:T(128)S(1)}, f32[40]{0:T(128)S(1)}, u32[]{:S(2)}, u32[]{:S(2)}) %collective-permute-start.3) | collective-permute-done | bytes 192 | tf_op jit(solution)/shard_map/ppermute | solution.py:15
  196.0 4.3 add_select_fusion.22
  200.3 6.4 collective-permute-start.15
  206.9 5.7 collective-permute-start.5
  212.7 107.4 %collective-permute-done.5 = f32[40]{0:T(128)S(1)} collective-permute-done((f32[40]{0:T(128)S(1)}, f32[40]{0:T(128)S(1)}, u32[]{:S(2)}, u32[]{:S(2)}) %collective-permute-start.5) | collective-permute-done | bytes 192 | tf_op jit(solution)/shard_map/ppermute | solution.py:15
  320.3 4.3 add_select_fusion.21
  327.4 54.2 %collective-permute-done.7 = f32[40]{0:T(128)S(1)} collective-permute-done((f32[40]{0:T(128)S(1)}, f32[40]{0:T(128)S(1)}, u32[]{:S(2)}, u32[]{:S(2)}) %collective-permute-start.7) | collective-permute-done | bytes 192 | tf_op jit(solution)/shard_map/ppermute | solution.py:15
  381.7 4.3 add_select_fusion.20
  386.0 2.7 collective-permute-start.17
  390.7 2.8 collective-permute-start.9
  394.2 49.3 %collective-permute-done.9 = f32[40]{0:T(128)S(1)} collective-permute-done((f32[40]{0:T(128)S(1)}, f32[40]{0:T(128)S(1)}, u32[]{:S(2)}, u32[]{:S(2)}) %collective-permute-start.9) | collective-permute-done | bytes 192 | tf_op jit(solution)/shard_map/ppermute | solution.py:15
  443.7 4.2 add_select_fusion.19
  449.5 1.8 broadcast.94.clone
  452.6 161.4 %while.34 = (s32[]{:T(128)}, f32[256,256]{1,0:T(8,128)S(1)}, f32[20,2,256]{2,1,0:T(2,128)}, f32[20,2,256]{2,1,0:T(2,128)}, f32[20,256,128]{1,2,0:T(8,128)}, /*in...) while((s32[]{:T(128)}, f32[256,256]{1,0:T(8,128)S(1)}, ...), condition=%wide.region_11.13_spmd.clone, body=%wide.region_6.12_spmd.clone.sunk | while | flops 203816448 | bytes 4162763 | solution.py:76
  619.2 4.3 add_select_fusion.18
  623.5 2.9 collective-permute-start.12
  626.6 1.8 broadcast.94.clone.1
  628.4 61.5 %while.33 = (s32[]{:T(128)}, f32[20,256,128]{1,2,0:T(8,128)}, f32[20,256,128]{1,2,0:T(8,128)S(1)}, f32[20,2,256]{2,1,0:T(2,128)}, f32[1,256,256]{2,1,0:T(8,128)}...) while((s32[]{:T(128)}, f32[20,256,128]{1,2,0:T(8,128)}, ...), condition=%wide.region_4.6_spmd.clone, body=%wide.region_3.5_spmd.clone.sunk | while | flops 101187584 | bytes 1127005 | solution.py:76
  638.3 1.7 fusion.106
  641.4 1.7 fusion.106
  644.5 1.7 fusion.106
  650.6 1.7 fusion.106
  653.7 1.7 fusion.106
  659.8 1.7 fusion.106
  672.1 1.7 fusion.106
  675.2 1.7 fusion.106
  681.4 1.7 fusion.106
  691.6 2.5 reduce-window.34
  699.9 9.6 %multiply_reduce_fusion.2 = (f32[2560]{0:T(1024)}, f32[128,2560]{0,1:T(8,128)S(1)}, f32[128,2560]{0,1:T(8,128)S(1)}) fusion(f32[128,2560]{0,1:T(8,128)} %collective-permute-done.13, pred[]{:T(512)S(6)} %eq.109, f32[128,2560]{0,1:T(8,128)} %collective-permute-done.14, f32[2560]{0:T(1024)S(1)} %mul.815, pred[]{:T(512)S(6)} %eq.108, ...), kind=kLoop, calls=%fused_computation.77 | loop fusion | flops 13104640 | bytes 21104654 | tf_op jit(solution)/shard_map/reduce_sum | solution.py:183
  711.2 6.5 bitcast_multiply_fusion.7
  717.8 2.0 reduce_sum.240
  721.9 2.5 reduce-window.36
  725.4 2.0 reduce_sum.239
  727.6 2.5 reduce-window.30
  732.6 2.4 copy.127
  735.0 2.6 copy.128
  737.8 6.8 fusion.38
  744.6 5.0 fusion.39
  749.6 82.6 %all-reduce.2 = (f32[40]{0:T(128)}, f32[40]{0:T(128)}, f32[40]{0:T(128)}) all-reduce(f32[40]{0:T(128)S(1)} %get-tuple-element.545, f32[40]{0:T(128)S(1)} %get-tuple-element.544, f32[40]{0:T(128)S(1)} %reduce_sum.252), channel_id=1, replica_groups=mesh['dp'=2,'ctx'=128] {'dp','ctx'}, use_global_device_ids=true, to_apply=%region_26.28 | all-reduce | flops 120 | bytes 960 | tf_op jit(solution)/shard_map/psum | solution.py:189
  (522 shorter events, 253.1 us)
Async XLA Ops:
  0.6 13.5 %copy-start = (bf16[1,256,128]{2,1,0:T(8,128)(2,1)S(1)}, bf16[1,256,128]{2,1,0:T(8,128)(2,1)}, u32[]{:S(2)}) copy-start(bf16[1,256,128]{2,1,0:T(8,128)(2,1)} %param.15) | copy-start | bytes 196612
  0.6 10.2 %copy-start.7 = (bf16[1,256,2560]{2,1,0:T(8,128)(2,1)S(1)}, bf16[1,256,2560]{2,1,0:T(8,128)(2,1)}, u32[]{:S(2)}) copy-start(bf16[1,256,2560]{2,1,0:T(8,128)(2,1)} %param.14) | copy-start | bytes 3932164
  7.8 381.1 %copy-start.15 = (f32[40,2]{0,1:T(2,128)}, f32[40,2]{0,1:T(2,128)S(1)}, u32[]{:S(2)}) copy-start(f32[40,2]{0,1:T(2,128)S(1)} %slice.33) | copy-start | bytes 964
  10.0 9.0 %copy-start.20 = (f32[256]{0:T(256)}, f32[256]{0:T(256)S(1)}, u32[]{:S(2)}) copy-start(f32[256]{0:T(256)S(1)} %get-tuple-element.543) | copy-start | bytes 3076
  16.5 58.5 %collective-permute-start = (f32[128,2560]{0,1:T(8,128)}, f32[128,2560]{0,1:T(8,128)}, u32[]{:S(2)}, u32[]{:S(2)}) collective-permute-start(f32[128,2560]{0,1:T(8,128)} %convolution_bitcast_fusion.3), channel_id=1, source_target_pairs={{0,1},{1,0},{2,3},{3,2},{4,5},{5,4},{6,7},{7,6},{8,9},{9,8},{10,11... | collective-permute-start | bytes 3932168 | tf_op jit(solution)/shard_map/ppermute | solution.py:15
  26.9 48.1 %collective-permute-start.13 = (f32[128,2560]{0,1:T(8,128)}, f32[128,2560]{0,1:T(8,128)}, u32[]{:S(2)}, u32[]{:S(2)}) collective-permute-start(f32[128,2560]{0,1:T(8,128)} %convolution_bitcast_fusion.2), channel_id=1, source_target_pairs={{0,1},{1,0},{2,3},{3,2},{4,5},{5,4},{6,7},{7,6},{8,9},{9,8},{10,11... | collective-permute-start | bytes 3932168 | tf_op jit(solution)/shard_map/ppermute | solution.py:15
  28.2 46.6 %collective-permute-start.1 = (f32[40]{0:T(128)S(1)}, f32[40]{0:T(128)S(1)}, u32[]{:S(2)}, u32[]{:S(2)}) collective-permute-start(f32[40]{0:T(128)S(1)} %exponential_multiply_fusion), channel_id=1, source_target_pairs={{0,1},{1,0},{2,3},{3,2},{4,5},{5,4},{6,7},{7,6},{8,9},{9,8},{10,11... | collective-permute-start | bytes 488 | tf_op jit(solution)/shard_map/ppermute | solution.py:15
  74.8 8.4 %copy-start.26 = (f32[40]{0:T(128)}, f32[40]{0:T(128)S(1)}, u32[]{:S(2)}) copy-start(f32[40]{0:T(128)S(1)} %collective-permute-done.1) | copy-start | bytes 484
  79.2 116.8 %collective-permute-start.14 = (f32[128,2560]{0,1:T(8,128)}, f32[128,2560]{0,1:T(8,128)}, u32[]{:S(2)}, u32[]{:S(2)}) collective-permute-start(f32[128,2560]{0,1:T(8,128)} %get-tuple-element.535), channel_id=1, source_target_pairs={{0,2},{1,3},{2,0},{3,1},{4,6},{5,7},{6,4},{7,5},{8,10},{9,11},{10,... | collective-permute-start | bytes 3932168 | tf_op jit(solution)/shard_map/ppermute | solution.py:15
  83.1 112.9 %collective-permute-start.2 = (f32[128,2560]{0,1:T(8,128)}, f32[128,2560]{0,1:T(8,128)}, u32[]{:S(2)}, u32[]{:S(2)}) collective-permute-start(f32[128,2560]{0,1:T(8,128)} %get-tuple-element.534), channel_id=1, source_target_pairs={{0,2},{1,3},{2,0},{3,1},{4,6},{5,7},{6,4},{7,5},{8,10},{9,11},{10,... | collective-permute-start | bytes 3932168 | tf_op jit(solution)/shard_map/ppermute | solution.py:15
  83.2 112.7 %collective-permute-start.3 = (f32[40]{0:T(128)S(1)}, f32[40]{0:T(128)S(1)}, u32[]{:S(2)}, u32[]{:S(2)}) collective-permute-start(f32[40]{0:T(128)S(1)} %fusion.87), channel_id=1, source_target_pairs={{0,2},{1,3},{2,0},{3,1},{4,6},{5,7},{6,4},{7,5},{8,10},{9,11},{10,... | collective-permute-start | bytes 488 | tf_op jit(solution)/shard_map/ppermute | solution.py:15
  195.9 11.0 %copy-start.28 = (f32[40]{0:T(128)}, f32[40]{0:T(128)S(1)}, u32[]{:S(2)}) copy-start(f32[40]{0:T(128)S(1)} %collective-permute-done.3) | copy-start | bytes 484
  200.3 119.9 %collective-permute-start.15 = (f32[128,2560]{0,1:T(8,128)}, f32[128,2560]{0,1:T(8,128)}, u32[]{:S(2)}, u32[]{:S(2)}) collective-permute-start(f32[128,2560]{0,1:T(8,128)} %get-tuple-element.533), channel_id=1, source_target_pairs={{0,4},{1,5},{2,6},{3,7},{4,0},{5,1},{6,2},{7,3},{8,12},{9,13},{10,... | collective-permute-start | bytes 3932168 | tf_op jit(solution)/shard_map/ppermute | solution.py:15
  206.8 113.5 %collective-permute-start.4 = (f32[128,2560]{0,1:T(8,128)}, f32[128,2560]{0,1:T(8,128)}, u32[]{:S(2)}, u32[]{:S(2)}) collective-permute-start(f32[128,2560]{0,1:T(8,128)} %get-tuple-element.532), channel_id=1, source_target_pairs={{0,4},{1,5},{2,6},{3,7},{4,0},{5,1},{6,2},{7,3},{8,12},{9,13},{10,... | collective-permute-start | bytes 3932168 | tf_op jit(solution)/shard_map/ppermute | solution.py:15
  206.9 113.2 %collective-permute-start.5 = (f32[40]{0:T(128)S(1)}, f32[40]{0:T(128)S(1)}, u32[]{:S(2)}, u32[]{:S(2)}) collective-permute-start(f32[40]{0:T(128)S(1)} %mul.725), channel_id=1, source_target_pairs={{0,4},{1,5},{2,6},{3,7},{4,0},{5,1},{6,2},{7,3},{8,12},{9,13},{10,... | collective-permute-start | bytes 488 | tf_op jit(solution)/shard_map/ppermute | solution.py:15
  320.1 5.9 copy-start.30
  324.5 57.1 %collective-permute-start.16 = (f32[128,2560]{0,1:T(8,128)}, f32[128,2560]{0,1:T(8,128)}, u32[]{:S(2)}, u32[]{:S(2)}) collective-permute-start(f32[128,2560]{0,1:T(8,128)} %get-tuple-element.531), channel_id=1, source_target_pairs={{0,8},{1,9},{2,10},{3,11},{4,12},{5,13},{6,14},{7,15},{8,0},{9,1},... | collective-permute-start | bytes 3932168 | tf_op jit(solution)/shard_map/ppermute | solution.py:15
  325.7 55.9 %collective-permute-start.6 = (f32[128,2560]{0,1:T(8,128)}, f32[128,2560]{0,1:T(8,128)}, u32[]{:S(2)}, u32[]{:S(2)}) collective-permute-start(f32[128,2560]{0,1:T(8,128)} %get-tuple-element.530), channel_id=1, source_target_pairs={{0,8},{1,9},{2,10},{3,11},{4,12},{5,13},{6,14},{7,15},{8,0},{9,1},... | collective-permute-start | bytes 3932168 | tf_op jit(solution)/shard_map/ppermute | solution.py:15
  326.0 55.5 %collective-permute-start.7 = (f32[40]{0:T(128)S(1)}, f32[40]{0:T(128)S(1)}, u32[]{:S(2)}, u32[]{:S(2)}) collective-permute-start(f32[40]{0:T(128)S(1)} %mul.732), channel_id=1, source_target_pairs={{0,8},{1,9},{2,10},{3,11},{4,12},{5,13},{6,14},{7,15},{8,0},{9,1},... | collective-permute-start | bytes 488 | tf_op jit(solution)/shard_map/ppermute | solution.py:15
  381.5 9.1 %copy-start.32 = (f32[40]{0:T(128)}, f32[40]{0:T(128)S(1)}, u32[]{:S(2)}) copy-start(f32[40]{0:T(128)S(1)} %collective-permute-done.7) | copy-start | bytes 484
  386.0 57.7 %collective-permute-start.17 = (f32[128,2560]{0,1:T(8,128)}, f32[128,2560]{0,1:T(8,128)}, u32[]{:S(2)}, u32[]{:S(2)}) collective-permute-start(f32[128,2560]{0,1:T(8,128)} %get-tuple-element.529), channel_id=1, source_target_pairs={{0,16},{1,17},{2,18},{3,19},{4,20},{5,21},{6,22},{7,23},{8,24},{9,... | collective-permute-start | bytes 3932168 | tf_op jit(solution)/shard_map/ppermute | solution.py:15
  388.7 55.0 %collective-permute-start.8 = (f32[128,2560]{0,1:T(8,128)}, f32[128,2560]{0,1:T(8,128)}, u32[]{:S(2)}, u32[]{:S(2)}) collective-permute-start(f32[128,2560]{0,1:T(8,128)} %get-tuple-element.528), channel_id=1, source_target_pairs={{0,16},{1,17},{2,18},{3,19},{4,20},{5,21},{6,22},{7,23},{8,24},{9,... | collective-permute-start | bytes 3932168 | tf_op jit(solution)/shard_map/ppermute | solution.py:15
  390.7 57.3 %copy-start.39 = (f32[40]{0:T(128)}, f32[40]{0:T(128)S(1)}, u32[]{:S(2)}) copy-start(f32[40]{0:T(128)S(1)} %mul.739) | copy-start | bytes 484
  390.7 52.9 %collective-permute-start.9 = (f32[40]{0:T(128)S(1)}, f32[40]{0:T(128)S(1)}, u32[]{:S(2)}, u32[]{:S(2)}) collective-permute-start(f32[40]{0:T(128)S(1)} %mul.739), channel_id=1, source_target_pairs={{0,16},{1,17},{2,18},{3,19},{4,20},{5,21},{6,22},{7,23},{8,24},{9,... | collective-permute-start | bytes 488 | tf_op jit(solution)/shard_map/ppermute | solution.py:15
  447.9 171.2 %collective-permute-start.10 = (f32[128,2560]{0,1:T(8,128)}, f32[128,2560]{0,1:T(8,128)}, u32[]{:S(2)}, u32[]{:S(2)}) collective-permute-start(f32[128,2560]{0,1:T(8,128)} %get-tuple-element.526), channel_id=1, source_target_pairs={{0,32},{1,33},{2,34},{3,35},{4,36},{5,37},{6,38},{7,39},{8,40},{9,... | collective-permute-start | bytes 3932168 | tf_op jit(solution)/shard_map/ppermute | solution.py:15
  449.3 169.8 %collective-permute-start.18 = (f32[128,2560]{0,1:T(8,128)}, f32[128,2560]{0,1:T(8,128)}, u32[]{:S(2)}, u32[]{:S(2)}) collective-permute-start(f32[128,2560]{0,1:T(8,128)} %get-tuple-element.527), channel_id=1, source_target_pairs={{0,32},{1,33},{2,34},{3,35},{4,36},{5,37},{6,38},{7,39},{8,40},{9,... | collective-permute-start | bytes 3932168 | tf_op jit(solution)/shard_map/ppermute | solution.py:15
  452.6 4.7 copy-start.13
  460.7 4.7 copy-start.13
  476.8 4.8 copy-start.13
  484.9 4.7 copy-start.13
  557.5 4.7 copy-start.13
  581.7 4.7 copy-start.13
  597.8 4.7 copy-start.13
  616.1 2.4 collective-permute-start.11
  623.5 76.4 %collective-permute-start.12 = (f32[128,2560]{0,1:T(8,128)}, f32[128,2560]{0,1:T(8,128)}, u32[]{:S(2)}, u32[]{:S(2)}) collective-permute-start(f32[128,2560]{0,1:T(8,128)} %get-tuple-element.524), channel_id=1, source_target_pairs={{0,64},{1,65},{2,66},{3,67},{4,68},{5,69},{6,70},{7,71},{8,72},{9,... | collective-permute-start | bytes 3932168 | tf_op jit(solution)/shard_map/ppermute | solution.py:15
  626.3 73.5 %collective-permute-start.19 = (f32[128,2560]{0,1:T(8,128)}, f32[128,2560]{0,1:T(8,128)}, u32[]{:S(2)}, u32[]{:S(2)}) collective-permute-start(f32[128,2560]{0,1:T(8,128)} %get-tuple-element.525), channel_id=1, source_target_pairs={{0,64},{1,65},{2,66},{3,67},{4,68},{5,69},{6,70},{7,71},{8,72},{9,... | collective-permute-start | bytes 3932168 | tf_op jit(solution)/shard_map/ppermute | solution.py:15
  689.9 7.7 copy-start.9
  689.9 8.1 copy-start.27
  689.9 8.1 copy-start.29
  689.9 8.1 copy-start.31
  689.9 8.1 copy-start.33
  689.9 8.1 copy-start.35
  689.9 8.1 copy-start.37
  699.8 10.9 %copy-start.4 = (f32[20,256,128]{1,2,0:T(8,128)S(1)}, f32[20,256,128]{1,2,0:T(8,128)}, u32[]{:S(2)}) copy-start(f32[20,256,128]{1,2,0:T(8,128)} %get-tuple-element.301) | copy-start | bytes 7864324
  699.9 10.8 %copy-start.5 = (f32[20,256,128]{1,2,0:T(8,128)S(1)}, f32[20,256,128]{1,2,0:T(8,128)}, u32[]{:S(2)}) copy-start(f32[20,256,128]{1,2,0:T(8,128)} %get-tuple-element.300) | copy-start | bytes 7864324
  725.4 5.1 copy-start.23
  737.8 6.8 copy-start.6
  744.6 5.0 copy-start.38
  (31 other events, 100.2 us)
where the time goes:
time: 844 us; the launch traced here: 832 us
  waiting for transfers between devices  367 us (43%)
  local copies, waits for them, and re-layouts  129 us (15%)
  matrix products  121 us (14%)
  other arithmetic  93.1 us (11%)
  blocking collectives  82.6 us (10%)
  starting transfers between devices  37 us (4%)
    ppermute x20, waiting for transfers between devices, swapped(): return lax.ppermute(value, axis, pairs)  367 us
    dot_general x60, matrix products, intra_group(): result = jnp.einsum('htu,uhp->thp', mixing, per_head, precision=EXACT)  94.2 us
    psum x1, blocking collectives, local(): lax.psum((bias_main + bias_state, decay_main + decay_state, skip_total),...  82.6 us
    dynamic_update_slice x60, local copies, waits for them, and re-layouts, block_main(): lax.map(jax.checkpoint(one_group), (cum_stack, stride_stack, feature_stack))  51.6 us
    ppermute x20, starting transfers between devices, swapped(): return lax.ppermute(value, axis, pairs)  37 us
    squeeze x40, local copies, waits for them, and re-layouts, block_main(): lax.map(jax.checkpoint(one_group), (cum_stack, stride_stack, feature_stack))  33.1 us
    select_n x7, other arithmetic, select_pair(): jnp.where(condition, left, right)  25.7 us
    and x21, other arithmetic, block_main(): (segment[:, None] == segment[None, :]) & (ordinal[:, None] >= ordinal[Non...  18.2 us
  transfers between devices with their start and end apart: 20, of which 6 were waited for; matrix products, arithmetic and copies ran while one was open for 30% of the time, Pallas kernels for 0%

commit v1 on v0

v1 whole, which is shorter than its diff:
```python
import functools

import jax
import jax.numpy as jnp
from jax import lax
from jax.experimental import pallas as pl
from jax.experimental.pallas import tpu as pltpu
from jax.sharding import PartitionSpec as P

MESH = pl.DeviceIdType.MESH
F32 = jnp.float32
BF16 = jnp.bfloat16
EXACT = lax.Precision.HIGHEST

HEADS = 40
PAIRS = 20
PAD = 24
HALF = 64
LEN = 256
WIDE = 2560
CHUNKS = 40
NY, NX, NZ = 4, 4, 8
HOP = 2
NEG = -1e30


def split2(value):
    high = value.astype(BF16)
    return high, (value - high.astype(F32)).astype(BF16)


def split3(value):
    high = value.astype(BF16)
    rest = value - high.astype(F32)
    middle = rest.astype(BF16)
    return high, middle, (rest - middle.astype(F32)).astype(BF16)


def mm(left, right):
    return jnp.dot(left, right, preferred_element_type=F32)


def mm_nt(left, right):
    return lax.dot_general(left, right, (((1,), (1,)), ((), ())), preferred_element_type=F32)


def mm_tn(left, right):
    return lax.dot_general(left, right, (((0,), (0,)), ((), ())), preferred_element_type=F32)


def iota(shape, axis):
    return lax.broadcasted_iota(jnp.int32, shape, axis)


def to_column(row):
    size = row.shape[1]
    eye = iota((size, size), 0) == iota((size, size), 1)
    return jnp.sum(jnp.where(eye, row, 0.0), axis=1, keepdims=True)


def to_row(column):
    size = column.shape[0]
    eye = iota((size, size), 0) == iota((size, size), 1)
    return jnp.sum(jnp.where(eye, column, 0.0), axis=0, keepdims=True)


def pair_rows(column):
    wide = jnp.broadcast_to(column, (HEADS, 128))
    head = iota((PAD, HEADS), 1)
    row = iota((PAD, HEADS), 0)
    even = jnp.dot((head == 2 * row).astype(F32), wide, precision=EXACT, preferred_element_type=F32)
    odd = jnp.dot((head == 2 * row + 1).astype(F32), wide, precision=EXACT, preferred_element_type=F32)
    return jnp.where(iota((PAD, 128), 1) < HALF, even, odd)


def unpair_sums(rows):
    first = jnp.sum(jnp.where(iota((PAD, 128), 1) < HALF, rows, 0.0), axis=1, keepdims=True)
    second = jnp.sum(jnp.where(iota((PAD, 128), 1) < HALF, 0.0, rows), axis=1, keepdims=True)
    head = iota((HEADS, PAD), 0)
    row = iota((HEADS, PAD), 1)
    first = jnp.broadcast_to(first, (PAD, 128))
    second = jnp.broadcast_to(second, (PAD, 128))
    total = jnp.dot((head == 2 * row).astype(F32), first, precision=EXACT, preferred_element_type=F32)
    total += jnp.dot((head == 2 * row + 1).astype(F32), second, precision=EXACT, preferred_element_type=F32)
    return total[:, 0:1]


def spread_columns(rows):
    high, middle, low = split3(rows)
    head = iota((HEADS, WIDE), 0)
    lane = iota((HEADS, WIDE), 1)
    expand = (lane // HALF == head).astype(BF16)
    return mm_tn(high, expand) + (mm_tn(middle, expand) + mm_tn(low, expand))


def steps(logits, bias_row, decay_row):
    bias = to_column(bias_row)
    rate = -jnp.exp(to_column(decay_row))
    shifted = logits + bias
    stride = jnp.maximum(shifted, 0.0) + jnp.log1p(jnp.exp(-jnp.abs(shifted)))
    return shifted, stride, rate


def before_kernel(
    docs_ref,
    x_ref,
    dy_ref,
    b_ref,
    c_ref,
    logit_ref,
    bias_ref,
    decay_ref,
    state_ref,
    lam_ref,
    y_ref,
    dx_ref,
    dg_ref,
    wide_w,
    wide_f,
    wide_l,
    wide_m,
    row_l,
    row_m,
    gram,
    gram_t,
    mask,
    mask_t,
    b_t,
    c_t,
):
    position = lax.axis_index("ctx")
    start = position * LEN
    shifted, stride, rate = steps(logit_ref[...], bias_ref[...], decay_ref[...])
    upper = (iota((LEN, LEN), 0) <= iota((LEN, LEN), 1)).astype(F32)
    total = jnp.dot(stride * rate, upper, precision=EXACT, preferred_element_type=F32)
    last = total[:, LEN - 1 : LEN]

    seg_row = jnp.zeros((1, LEN), jnp.int32)
    seg_col = jnp.zeros((LEN, 128), jnp.int32)
    entry = jnp.int32(0)
    final = jnp.int32(0)
    for d in range(docs_ref.shape[1]):
        doc = docs_ref[0, d] - start
        seg_row += (doc <= iota((1, LEN), 1)).astype(jnp.int32)
        seg_col += (doc <= iota((LEN, 128), 0)).astype(jnp.int32)
        entry += (doc <= -1).astype(jnp.int32)
        final += (doc <= LEN - 1).astype(jnp.int32)
    seg_col = seg_col[:, 0:1]
    same = seg_col == seg_row
    mask[...] = jnp.where(same & (iota((LEN, LEN), 0) >= iota((LEN, LEN), 1)), 0.0, NEG)
    mask_t[...] = jnp.where(same & (iota((LEN, LEN), 0) <= iota((LEN, LEN), 1)), 0.0, NEG)
    keep = (seg_row == entry).astype(F32)
    own = (seg_row == final).astype(F32)
    linked = (final == entry).astype(F32)

    weight = own * jnp.exp(last - total) * stride
    factor = keep * jnp.exp(total)
    moved = total - jnp.log(stride)
    row_l[...] = total
    row_m[...] = moved
    wide_w[...] = spread_columns(weight)
    wide_f[...] = spread_columns(factor)
    wide_l[...] = spread_columns(total)
    wide_m[...] = spread_columns(moved)
    lam_ref[...] = pair_rows(jnp.exp(last) * linked)

    b = b_ref[...]
    c = c_ref[...]
    gram[...] = mm_nt(c, b)
    gram_t[...] = mm_nt(b, c)
    b_t[...] = b.astype(F32).T.astype(BF16)
    c_t[...] = c.astype(F32).T.astype(BF16)
    dg_ref[...] = jnp.zeros((LEN, LEN), F32)

    def pair(j, carry):
        lanes = pl.ds(pl.multiple_of(j * 128, 128), 128)
        x = x_ref[:, lanes]
        dy = dy_ref[:, lanes]
        first = iota((LEN, 128), 1) < HALF
        high, low = split2(wide_w[:, lanes] * x.astype(F32))
        state = mm(b_t[...], high) + mm(b_t[...], low)
        high, low = split2(wide_f[:, lanes] * dy.astype(F32))
        state_b = mm(c_t[...], high) + mm(c_t[...], low)
        state_ref[2 * j, 0] = state[:HALF]
        state_ref[2 * j + 1, 0] = state[HALF:]
        state_ref[2 * j, 1] = state_b[:HALF]
        state_ref[2 * j + 1, 1] = state_b[HALF:]
        columns_l = wide_l[:, lanes]
        columns_m = wide_m[:, lanes]
        ys, dxs = [], []
        for k in range(2):
            lrow = row_l[pl.ds(2 * j + k, 1), :]
            mrow = row_m[pl.ds(2 * j + k, 1), :]
            lcol = columns_l[:, k * HALF : k * HALF + 1]
            mcol = columns_m[:, k * HALF : k * HALF + 1]
            decays = jnp.exp((lcol - mrow) + mask[...])
            high, low = split2(decays * gram[...])
            ys.append(mm(high, x) + mm(low, x))
            part = jnp.where(first if k == 0 else ~first, dy, jnp.zeros_like(dy))
            dg_ref[...] += mm_nt(part, x) * decays
            decays_t = jnp.exp((lrow - mcol) + mask_t[...])
            high, low = split2(decays_t * gram_t[...])
            dxs.append(mm(high, dy) + mm(low, dy))
        y_ref[:, lanes] = jnp.where(first, ys[0], ys[1])
        dx_ref[:, lanes] = jnp.where(first, dxs[0], dxs[1])
        return carry

    lax.fori_loop(0, PAIRS, pair, 0)


def place():
    index = lax.axis_index("ctx")
    return index // (NX * NZ), (index // NZ) % NX, index % NZ


def at(y, x, z):
    return (lax.axis_index("dp"), (y * NX + x) * NZ + z)


def partner(i):
    return i + 1 - 2 * (i % 2)


def scan_kernel(
    state_ref,
    lam_ref,
    out_ref,
    up_in,
    up_out,
    down_in,
    down_out,
    t_out,
    x1_in,
    u2_out,
    x2_in,
    u_out,
    y1_in,
    v2_out,
    y2_in,
    zlam,
    xlam,
    ylam,
    coef,
    send_sem,
    recv_sem,
    small_send,
    small_recv,
):
    y, x, z = place()
    barrier = pltpu.get_barrier_semaphore()
    peers = [at(y, x, (z + k) % NZ) for k in range(1, NZ)]
    peers += [at(y, (x + k) % NX, z) for k in range(1, NX)]
    peers += [at((y + k) % NY, x, z) for k in range(1, NY)]
    for peer in peers:
        pl.semaphore_signal(barrier, inc=1, device_id=peer, device_id_type=MESH)
    pl.semaphore_wait(barrier, len(peers))

    def gather(table, own, size, value, targets, offset):
        table[own] = value
        copies = []
        for k, target in enumerate(targets):
            copy = pltpu.make_async_remote_copy(
                src_ref=table.at[own],
                dst_ref=table.at[own],
                send_sem=small_send.at[offset + k],
                recv_sem=small_recv.at[offset + k],
                device_id=target,
                device_id_type=MESH,
            )
            copy.start()
            copies.append(copy)
        for k, copy in enumerate(copies):
            source = (own + size - 1 - k) % size
            pltpu.make_async_remote_copy(
                src_ref=table.at[source],
                dst_ref=table.at[source],
                send_sem=small_send.at[offset + k],
                recv_sem=small_recv.at[offset + k],
                device_id=targets[k],
                device_id_type=MESH,
            ).wait_recv()
        for copy in copies:
            copy.wait_send()

    one = jnp.ones((PAD, 128), F32)
    zero = jnp.zeros((PAD, 128), F32)

    def products(table, own, size):
        below, above = one, one
        for k in range(size):
            below *= jnp.where(own > k, table[k], one)
            above *= jnp.where(own < k, table[k], one)
        return below, above

    gather(zlam, z, NZ, lam_ref[...], peers[:7], 0)
    below_z, above_z = products(zlam, z, NZ)
    group = below_z * above_z * lam_ref[...]
    gather(xlam, x, NX, group, peers[7:10], 7)
    below_x, above_x = products(xlam, x, NX)
    plane = below_x * above_x * group
    gather(ylam, y, NY, plane, peers[10:13], 10)

    def ring_of_four(table, own):
        mine, other = table[own], table[partner(own)]
        both = mine * other
        across = table[3 - own] * table[partner(3 - own)]
        odd = own % 2 == 1
        upper = own >= 2
        forward = (
            jnp.where(odd, one, other),
            jnp.where(odd, mine, one),
            jnp.where(odd, one, zero),
            jnp.where(upper, one, across),
            jnp.where(upper, both, one),
            jnp.where(upper, jnp.where(odd, other, one), zero),
        )
        backward = (
            jnp.where(odd, other, one),
            jnp.where(odd, one, mine),
            jnp.where(odd, zero, one),
            jnp.where(upper, across, one),
            jnp.where(upper, one, both),
            jnp.where(upper, zero, jnp.where(odd, one, other)),
        )
        return forward, backward

    in_x = ring_of_four(xlam, x)
    in_y = ring_of_four(ylam, y)
    for d in range(2):
        outer, inner = (below_z, above_z) if d == 0 else (above_z, below_z)
        outer_x = outer * (below_x if d == 0 else above_x)
        table = (
            lam_ref[...],
            inner,
            in_x[d][0],
            in_x[d][1],
            in_x[d][3],
            in_x[d][4],
            in_y[d][0],
            in_y[d][1],
            outer * in_x[d][2],
            outer * in_x[d][5],
            outer_x * in_y[d][2],
            outer_x * in_y[d][5],
        )
        for k, value in enumerate(table):
            coef[d, k] = value

    @pl.when(z == 0)
    def _():
        up_in[...] = jnp.zeros_like(up_in)

    @pl.when(z == NZ - 1)
    def _():
        down_in[...] = jnp.zeros_like(down_in)

    to_up = at(y, x, (z + 1) % NZ)
    to_down = at(y, x, (z + NZ - 1) % NZ)
    to_x1 = at(y, partner(x), z)
    to_x2 = at(y, 3 - x, z)
    to_y1 = at(partner(y), x, z)
    to_y2 = at(3 - y, x, z)

    def link(stage, c, source, target, device):
        return pltpu.make_async_remote_copy(
            src_ref=source.at[c],
            dst_ref=target.at[c],
            send_sem=send_sem.at[stage, c],
            recv_sem=recv_sem.at[stage, c],
            device_id=device,
            device_id_type=MESH,
        )

    links = (
        functools.partial(link, 0, source=up_out, target=up_in, device=to_up),
        functools.partial(link, 1, source=down_out, target=down_in, device=to_down),
        functools.partial(link, 2, source=t_out, target=x1_in, device=to_x1),
        functools.partial(link, 3, source=u2_out, target=x2_in, device=to_x2),
        functools.partial(link, 4, source=u_out, target=y1_in, device=to_y1),
        functools.partial(link, 5, source=v2_out, target=y2_in, device=to_y2),
    )

    def staged(c):
        return (c >= 0) & (c < CHUNKS)

    lag_t = HOP * jnp.maximum(z, NZ - 1 - z)

    def tick(i, carry):
        def row(d, k, c):
            return coef[d, k, pl.ds(c // 2, 1), :]

        c_up = i - HOP * z

        @pl.when(staged(c_up))
        def _():
            @pl.when(z > 0)
            def _():
                links[0](c_up).wait_recv()

            up_out[c_up, 0] = row(0, 0, c_up) * up_in[c_up, 0] + state_ref[c_up, 0]
            up_out[c_up, 1] = up_in[c_up, 1] + row(1, 1, c_up) * state_ref[c_up, 1]

            @pl.when(z < NZ - 1)
            def _():
                links[0](c_up).start()

        c_down = i - HOP * (NZ - 1 - z)

        @pl.when(staged(c_down))
        def _():
            @pl.when(z < NZ - 1)
            def _():
                links[1](c_down).wait_recv()

            down_out[c_down, 0] = down_in[c_down, 0] + row(0, 1, c_down) * state_ref[c_down, 0]
            down_out[c_down, 1] = row(1, 0, c_down) * down_in[c_down, 1] + state_ref[c_down, 1]

            @pl.when(z > 0)
            def _():
                links[1](c_down).start()

        c_t = i - lag_t

        @pl.when(staged(c_t))
        def _():
            t_out[c_t, 0] = up_out[c_t, 0] * row(0, 1, c_t) + down_in[c_t, 0]
            t_out[c_t, 1] = down_out[c_t, 1] * row(1, 1, c_t) + up_in[c_t, 1]
            links[2](c_t).start()

        for stage, mine, came, result, k in (
            (2, t_out, x1_in, u2_out, 2),
            (3, u2_out, x2_in, u_out, 4),
            (4, u_out, y1_in, v2_out, 6),
        ):
            c = c_t - HOP * (stage - 1)

            @pl.when(staged(c))
            def _(stage=stage, mine=mine, came=came, result=result, k=k, c=c):
                links[stage](c).wait_recv()
                for d in range(2):
                    result[c, d] = row(d, k, c) * mine[c, d] + row(d, k + 1, c) * came[c, d]
                links[stage + 1](c).start()

        c_end = c_t - HOP * 4

        @pl.when(staged(c_end))
        def _():
            links[5](c_end).wait_recv()
            for d, near in ((0, up_in), (1, down_in)):
                out_ref[c_end, d] = near[c_end, d] + (
                    (row(d, 8, c_end) * x1_in[c_end, d] + row(d, 9, c_end) * x2_in[c_end, d])
                    + (row(d, 10, c_end) * y1_in[c_end, d] + row(d, 11, c_end) * y2_in[c_end, d])
                )

        return carry

    lax.fori_loop(0, CHUNKS + HOP * (NZ - 1 + 4), tick, 0)

    def drain(c, carry):
        @pl.when(z < NZ - 1)
        def _():
            links[0](c).wait_send()

        @pl.when(z > 0)
        def _():
            links[1](c).wait_send()

        for stage in range(2, 6):
            links[stage](c).wait_send()
        return carry

    lax.fori_loop(0, CHUNKS, drain, 0)


def after_kernel(
    docs_ref,
    x_ref,
    dy_ref,
    b_ref,
    c_ref,
    logit_ref,
    bias_ref,
    decay_ref,
    skip_ref,
    wide_w,
    wide_f,
    state_ref,
    lam_ref,
    in_ref,
    y_ref,
    dx_ref,
    dg_ref,
    mixed_ref,
    feature_ref,
    write_ref,
    read_ref,
    step_ref,
    sums_ref,
    db,
    dc,
    rows_r,
    rows_v,
    row_last,
    row_skip,
    gains,
):
    shifted, stride, rate = steps(logit_ref[...], bias_ref[...], decay_ref[...])
    gains[...] = pair_rows(to_column(skip_ref[...]))
    db[...] = jnp.zeros_like(db)
    dc[...] = jnp.zeros_like(dc)
    row_last[...] = jnp.zeros_like(row_last)
    row_skip[...] = jnp.zeros_like(row_skip)
    b = b_ref[...]
    c = c_ref[...]

    def pair(j, carry):
        lanes = pl.ds(pl.multiple_of(j * 128, 128), 128)
        x = x_ref[:, lanes]
        dy = dy_ref[:, lanes]
        x32 = x.astype(F32)
        dy32 = dy.astype(F32)
        w = wide_w[:, lanes]
        f = wide_f[:, lanes]
        gain = gains[pl.ds(j, 1), :]
        state_in = jnp.concatenate([in_ref[2 * j, 0], in_ref[2 * j + 1, 0]], axis=0)
        adjoint = jnp.concatenate([in_ref[2 * j, 1], in_ref[2 * j + 1, 1]], axis=0)
        state_end = jnp.concatenate([state_ref[2 * j, 0], state_ref[2 * j + 1, 0]], axis=0)
        s_high, s_low = split2(state_in)
        a_high, a_low = split2(adjoint)
        y = y_ref[:, lanes] + f * (mm(c, s_high) + mm(c, s_low))
        dx = dx_ref[:, lanes] + w * (mm(b, a_high) + mm(b, a_low))
        mixed_ref[:, lanes] = (y + gain * x32).astype(BF16)
        feature_ref[:, lanes] = (dx + gain * dy32).astype(BF16)
        select = (iota((8, 128), 1) // HALF == iota((8, 128), 0)).astype(BF16)
        high, middle, low = split3(dy32 * y)
        r = mm_nt(select, high) + (mm_nt(select, middle) + mm_nt(select, low))
        high, middle, low = split3(x32 * dx)
        v = mm_nt(select, high) + (mm_nt(select, middle) + mm_nt(select, low))
        for k in range(2):
            rows_r[pl.ds(2 * j + k, 1), :] = r[k : k + 1]
            rows_v[pl.ds(2 * j + k, 1), :] = v[k : k + 1]
        high, low = split2(f * dy32)
        dc[...] += mm_nt(high, s_high) + (mm_nt(high, s_low) + mm_nt(low, s_high))
        high, low = split2(w * x32)
        db[...] += mm_nt(high, a_high) + (mm_nt(high, a_low) + mm_nt(low, a_high))
        row_skip[pl.ds(j, 1), :] = jnp.sum(dy32 * x32, axis=0, keepdims=True)
        leaving = lam_ref[pl.ds(j, 1), :] * state_in + state_end
        row_last[pl.ds(j, 1), :] = jnp.sum(adjoint * leaving, axis=0, keepdims=True)
        return carry

    lax.fori_loop(0, PAIRS, pair, 0)
    dg = dg_ref[...]
    high, low = split2(dg)
    read_ref[...] = (dc[...] + (mm(high, b) + mm(low, b))).astype(BF16)
    high, low = split2(dg.T)
    write_ref[...] = (db[...] + (mm(high, c) + mm(low, c))).astype(BF16)

    v = rows_v[...]
    is_last = iota((HEADS, LEN), 1) == LEN - 1
    slope = rows_r[...] - v + jnp.where(is_last, unpair_sums(row_last[...]), 0.0)
    lower = (iota((LEN, LEN), 0) >= iota((LEN, LEN), 1)).astype(F32)
    slope = jnp.dot(slope, lower, precision=EXACT, preferred_element_type=F32)
    step = (v / stride + rate * slope) * (1.0 / (1.0 + jnp.exp(-shifted)))
    step_ref[...] = step
    bias_sum = jnp.sum(step, axis=1, keepdims=True)
    decay_sum = jnp.sum(slope * (rate * stride), axis=1, keepdims=True)
    skip_sum = unpair_sums(row_skip[...])
    sums_ref[...] = jnp.concatenate(
        [to_row(bias_sum), to_row(decay_sum), to_row(skip_sum), jnp.zeros((5, HEADS), F32)], axis=0
    )


VM = pl.BlockSpec(memory_space=pltpu.VMEM)
SM = pl.BlockSpec(memory_space=pltpu.SMEM)


def shape(dims, kind=F32):
    return jax.ShapeDtypeStruct(dims, kind)


def local(
    features,
    write_keys,
    read_queries,
    step_logits,
    step_bias,
    decay_log,
    skip_gain,
    doc_starts,
    out_grad,
):
    x, b, c, logits, dy = features[0], write_keys[0], read_queries[0], step_logits[0], out_grad[0]
    bias, decay, skip = step_bias[None], decay_log[None], skip_gain[None]
    carry_shape = (CHUNKS, 2, HALF, 128)
    state, lam, y, dx, dg, wide_w, wide_f = pl.pallas_call(
        before_kernel,
        out_shape=(
            shape(carry_shape),
            shape((PAD, 128)),
            shape((LEN, WIDE)),
            shape((LEN, WIDE)),
            shape((LEN, LEN)),
            shape((LEN, WIDE)),
            shape((LEN, WIDE)),
        ),
        in_specs=[SM] + [VM] * 7,
        out_specs=(VM,) * 7,
        scratch_shapes=[pltpu.VMEM((LEN, WIDE), F32)] * 2
        + [pltpu.VMEM((HEADS, LEN), F32)] * 2
        + [pltpu.VMEM((LEN, LEN), F32)] * 4
        + [pltpu.VMEM((128, LEN), BF16)] * 2,
        compiler_params=pltpu.CompilerParams(vmem_limit_bytes=56 * 2**20),
        name="before",
    )(doc_starts, x, dy, b, c, logits, bias, decay)
    entering = pl.pallas_call(
        scan_kernel,
        out_shape=shape(carry_shape),
        in_specs=[VM] * 2,
        out_specs=VM,
        scratch_shapes=[pltpu.VMEM(carry_shape, F32)] * 12
        + [pltpu.VMEM((NZ, PAD, 128), F32), pltpu.VMEM((NX, PAD, 128), F32), pltpu.VMEM((NY, PAD, 128), F32)]
        + [pltpu.VMEM((2, 12, PAD, 128), F32)]
        + [pltpu.SemaphoreType.DMA((6, CHUNKS))] * 2
        + [pltpu.SemaphoreType.DMA((13,))] * 2,
        compiler_params=pltpu.CompilerParams(
            collective_id=0, has_side_effects=True, vmem_limit_bytes=56 * 2**20
        ),
        name="scan",
    )(state, lam)
    mixed, feature_grad, write_grad, read_grad, step_grad, sums = pl.pallas_call(
        after_kernel,
        out_shape=(
            shape((LEN, WIDE), BF16),
            shape((LEN, WIDE), BF16),
            shape((LEN, 128), BF16),
            shape((LEN, 128), BF16),
            shape((HEADS, LEN)),
            shape((8, HEADS)),
        ),
        in_specs=[SM] + [VM] * 16,
        out_specs=(VM,) * 6,
        scratch_shapes=[pltpu.VMEM((LEN, 128), F32)] * 2
        + [pltpu.VMEM((HEADS, LEN), F32)] * 2
        + [pltpu.VMEM((PAD, 128), F32)] * 3,
        compiler_params=pltpu.CompilerParams(vmem_limit_bytes=56 * 2**20),
        name="after",
    )(doc_starts, x, dy, b, c, logits, bias, decay, skip, wide_w, wide_f, state, lam, entering, y, dx, dg)
    sums = lax.psum(sums, ("dp", "ctx"))
    return (
        mixed[None],
        feature_grad[None],
        write_grad[None],
        read_grad[None],
        step_grad[None],
        sums[0],
        sums[1],
        sums[2],
    )


def solution(mesh):
    in_specs = (
        P("dp", "ctx", None),
        P("dp", "ctx", None),
        P("dp", "ctx", None),
        P("dp", None, "ctx"),
        P(),
        P(),
        P(),
        P("dp", None),
        P("dp", "ctx", None),
    )
    out_specs = (
        P("dp", "ctx", None),
        P("dp", "ctx", None),
        P("dp", "ctx", None),
        P("dp", "ctx", None),
        P("dp", None, "ctx"),
        P(),
        P(),
        P(),
    )
    return jax.shard_map(local, mesh=mesh, in_specs=in_specs, out_specs=out_specs, check_vma=False)
```

time: 844 us -> 265 us (0.31); the launches traced: 832 us -> 265 us
  waiting for transfers between devices: 367 us -> 0 us
  Pallas kernels: 0 us -> 169 us
  local copies, waits for them, and re-layouts: 129 us -> 0.52 us
  matrix products: 121 us -> 0 us
  other arithmetic: 93.1 us -> 0 us
  starting transfers between devices: 37 us -> 0 us
  blocking collectives: 82.6 us -> 94.4 us
    ppermute x20 -> x0, waiting for transfers between devices: 367 us -> none  [swapped(): return lax.ppermute(value, axis, pairs)]
    pallas_call x0 -> x3, Pallas kernels: none -> 169 us  [the longest x1 121 us: local(): pl.pallas_call(scan_kernel, out_shape=shape(carry_shape), in_specs=[VM] *...]
    dot_general x69 -> x0, matrix products: 121 us -> none  [the longest x60 94.2 us: intra_group(): result = jnp.einsum('htu,uhp->thp', mixing, per_head, precision=EXACT)]
    dynamic_update_slice x60 -> x0, local copies, waits for them, and re-layouts: 51.6 us -> none  [block_main(): lax.map(jax.checkpoint(one_group), (cum_stack, stride_stack, feature_stack))]
    ppermute x20 -> x0, starting transfers between devices: 37 us -> none  [swapped(): return lax.ppermute(value, axis, pairs)]
    squeeze x40 -> x1, local copies, waits for them, and re-layouts: 33.1 us -> 0.52 us  [local(): sums[2]]
    select_n x8 -> x0, other arithmetic: 26.4 us -> none  [the longest x7 25.7 us: select_pair(): jnp.where(condition, left, right)]
    and x21 -> x0, other arithmetic: 18.2 us -> none  [block_main(): (segment[:, None] == segment[None, :]) & (ordinal[:, None] >= ordinal[Non...]
  transfers between devices with their start and end apart: 20 -> 0, of which waited for: 6 -> 0; matrix products, arithmetic and copies ran while one was open for 30% -> 0% of each run, Pallas kernels for 0% -> 0%
where the time goes in v1:
time: 265 us
  Pallas kernels  169 us (64%)
  blocking collectives  94.4 us (36%)
    pallas_call x1, Pallas kernels, local(): pl.pallas_call(scan_kernel, out_shape=shape(carry_shape), in_specs=[VM] *...  121 us
    psum x1, blocking collectives, local(): sums = lax.psum(sums, ('dp', 'ctx'))  94.4 us
    pallas_call x1, Pallas kernels, local(): pl.pallas_call(before_kernel, out_shape=(shape(carry_shape), shape((PAD,...  26.3 us
    pallas_call x1, Pallas kernels, local(): pl.pallas_call(after_kernel, out_shape=(shape((LEN, WIDE), BF16), shape((...  21.4 us

profile of v1, /device:TPU:1, one launch (start us, length us, event | category | flops | bytes accessed | tf_op | source)
XLA Modules:
  0.0 264.5 jit_solution(12683542279262264763)
XLA Ops:
  0.6 26.3 %before.1 = (f32[40,2,64,128]{3,2,1,0:T(8,128)}, f32[24,128]{1,0:T(8,128)}, f32[256,2560]{1,0:T(8,128)}, f32[256,2560]{1,0:T(8,128)}, f32[256,256]{1,0:T(8,128)}...) custom-call(s32[1,32]{1,0:T(1,128)} %docs_ref.3, bf16[256,2560]{1,0:T(8,128)(2,1)} %bitcast.19, bf16[256,2560]{1,0:T(8,128)(2,1)} %bitcast.21, ...), custom_call_target="tpu_custom_call" | custom-call | tf_op jit(solution)/shard_map/before/pallas_call | solution.py:595
  27.0 121.2 %scan.1.in_ref = f32[40,2,64,128]{3,2,1,0:T(8,128)} custom-call(f32[40,2,64,128]{3,2,1,0:T(8,128)} %get-tuple-element.23.state_ref, f32[24,128]{1,0:T(8,128)} %get-tuple-element.24.lam_ref), custom_call_target="tpu_custom_call" | custom-call | tf_op jit(solution)/shard_map/scan/pallas_call | solution.py:615
  148.2 21.4 %after.1 = (bf16[256,2560]{1,0:T(8,128)(2,1)}, bf16[256,2560]{1,0:T(8,128)(2,1)}, bf16[256,128]{1,0:T(8,128)(2,1)}, bf16[256,128]{1,0:T(8,128)(2,1)}, f32[40,256]{1,0:T(8,128)}, /*index=5*/f32[8,40]{1,0:T(8,128)}) custom-call(s32[1,32]{1,0:T(1,128)} %docs_ref.3, bf16[256,2560]{1,0:T(8,128)(2,1)} %bitcast.20, bf16[256,2560]{1,0:T(8,128)(2,1)} %bitcast.22, ...), custom_call_target="tpu_custom_call" | custom-call | tf_op jit(solution)/shard_map/after/pallas_call | solution.py:630
  169.6 94.4 %psum.7 = f32[8,40]{1,0:T(8,128)S(1)} all-reduce(f32[8,40]{1,0:T(8,128)} %get-tuple-element.33), channel_id=1, replica_groups=mesh['dp'=2,'ctx'=128] {'dp','ctx'}, use_global_device_ids=true, to_apply=%region_0.0 | all-reduce | flops 320 | bytes 2560 | tf_op jit(solution)/shard_map/psum | solution.py:648
  264.0 0.5 slice_bitcast_fusion

commit v2 on v1

v2 whole, which is shorter than its diff:
```python
import functools

import jax
import jax.numpy as jnp
from jax import lax
from jax.experimental import pallas as pl
from jax.experimental.pallas import tpu as pltpu
from jax.sharding import PartitionSpec as P

MESH = pl.DeviceIdType.MESH
F32 = jnp.float32
BF16 = jnp.bfloat16
EXACT = lax.Precision.HIGHEST

HEADS = 40
PAIRS = 20
PAD = 24
HALF = 64
LEN = 256
WIDE = 2560
CHUNKS = 40
SPLIT = CHUNKS // PAIRS
ROWS = 128 // SPLIT
NY, NX, NZ = 4, 4, 8
HOP = 3
GATHER_X = 3
GATHER_Y = 7
NEG = -1e30


def split2(value):
    high = value.astype(BF16)
    return high, (value - high.astype(F32)).astype(BF16)


def split3(value):
    high = value.astype(BF16)
    rest = value - high.astype(F32)
    middle = rest.astype(BF16)
    return high, middle, (rest - middle.astype(F32)).astype(BF16)


def mm(left, right):
    return jnp.dot(left, right, preferred_element_type=F32)


def mm_nt(left, right):
    return lax.dot_general(left, right, (((1,), (1,)), ((), ())), preferred_element_type=F32)


def mm_tn(left, right):
    return lax.dot_general(left, right, (((0,), (0,)), ((), ())), preferred_element_type=F32)


def iota(shape, axis):
    return lax.broadcasted_iota(jnp.int32, shape, axis)


def to_column(row):
    size = row.shape[1]
    eye = iota((size, size), 0) == iota((size, size), 1)
    return jnp.sum(jnp.where(eye, row, 0.0), axis=1, keepdims=True)


def to_row(column):
    size = column.shape[0]
    eye = iota((size, 128), 0) == iota((size, 128), 1)
    return jnp.sum(jnp.where(eye, column, 0.0), axis=0, keepdims=True)


def pair_rows(column):
    wide = jnp.broadcast_to(column, (HEADS, 128))
    head = iota((PAD, HEADS), 1)
    row = iota((PAD, HEADS), 0)
    even = jnp.dot((head == 2 * row).astype(F32), wide, precision=EXACT, preferred_element_type=F32)
    odd = jnp.dot((head == 2 * row + 1).astype(F32), wide, precision=EXACT, preferred_element_type=F32)
    return jnp.where(iota((PAD, 128), 1) < HALF, even, odd)


def unpair_sums(rows):
    first = jnp.sum(jnp.where(iota((PAD, 128), 1) < HALF, rows, 0.0), axis=1, keepdims=True)
    second = jnp.sum(jnp.where(iota((PAD, 128), 1) < HALF, 0.0, rows), axis=1, keepdims=True)
    head = iota((HEADS, PAD), 0)
    row = iota((HEADS, PAD), 1)
    first = jnp.broadcast_to(first, (PAD, 128))
    second = jnp.broadcast_to(second, (PAD, 128))
    total = jnp.dot((head == 2 * row).astype(F32), first, precision=EXACT, preferred_element_type=F32)
    total += jnp.dot((head == 2 * row + 1).astype(F32), second, precision=EXACT, preferred_element_type=F32)
    return total[:, 0:1]


def steps(logits, bias_row, decay_row):
    bias = to_column(bias_row)
    rate = -jnp.exp(to_column(decay_row))
    shifted = logits + bias
    stride = jnp.maximum(shifted, 0.0) + jnp.log1p(jnp.exp(-jnp.abs(shifted)))
    return shifted, stride, rate


def place():
    index = lax.axis_index("ctx")
    return index // (NX * NZ), (index // NZ) % NX, index % NZ


def at(y, x, z):
    return (lax.axis_index("dp"), (y * NX + x) * NZ + z)


def partner(i):
    return i + 1 - 2 * (i % 2)


def stacked(rows):
    parts = [part.astype(F32) for part in split3(rows)] + [jnp.zeros((8, LEN), F32)]
    return jnp.concatenate(parts, axis=0).T.astype(BF16)


def spread(j):
    line = iota((128, 128), 0)
    head = line - HEADS * ((line >= HEADS).astype(jnp.int32) + (line >= 2 * HEADS).astype(jnp.int32))
    return ((head == 2 * j + iota((128, 128), 1) // HALF) & (line < 3 * HEADS)).astype(BF16)


def layer_kernel(
    docs_ref,
    x_ref,
    dy_ref,
    b_ref,
    c_ref,
    logit_ref,
    bias_ref,
    decay_ref,
    skip_ref,
    mixed_ref,
    feature_ref,
    write_ref,
    read_ref,
    step_ref,
    bias_out,
    decay_out,
    skip_out,
    state_ref,
    up_in,
    up_out,
    down_in,
    down_out,
    t_out,
    x1_in,
    u2_out,
    x2_in,
    u_out,
    y1_in,
    v2_out,
    y2_in,
    zlam,
    xlam,
    ylam,
    coef,
    zsum,
    xsum,
    ysum,
    csum,
    wide_w,
    wide_f,
    y_ref,
    dx_ref,
    dg_ref,
    stack_w,
    stack_f,
    stack_l,
    stack_m,
    row_l,
    row_m,
    gram,
    gram_t,
    mask,
    mask_t,
    b_t,
    c_t,
    db,
    dc,
    rows_r,
    rows_v,
    row_last,
    row_skip,
    gains,
    lam_ref,
    send_sem,
    recv_sem,
    small_send,
    small_recv,
):
    y, x, z = place()
    core = lax.axis_index("dp")
    barrier = pltpu.get_barrier_semaphore()
    peers = [at(y, x, (z + k) % NZ) for k in range(1, NZ)]
    peers += [at(y, (x + k) % NX, z) for k in range(1, NX)]
    peers += [at((y + k) % NY, x, z) for k in range(1, NY)]
    peers += [(1 - core, lax.axis_index("ctx"))]
    for peer in peers:
        pl.semaphore_signal(barrier, inc=1, device_id=peer, device_id_type=MESH)

    def gather_copy(table, slot, target, k):
        return pltpu.make_async_remote_copy(
            src_ref=table.at[slot],
            dst_ref=table.at[slot],
            send_sem=small_send.at[k],
            recv_sem=small_recv.at[k],
            device_id=target,
            device_id_type=MESH,
        )

    def gather_start(table, own, value, targets, offset):
        table[own] = value
        for k, target in enumerate(targets):
            gather_copy(table, own, target, offset + k).start()

    def gather_end(table, own, size, targets, offset):
        for k, target in enumerate(targets):
            gather_copy(table, (own + size - 1 - k) % size, target, offset + k).wait_recv()
        for k, target in enumerate(targets):
            gather_copy(table, own, target, offset + k).wait_send()

    one = jnp.ones((PAD, 128), F32)
    zero = jnp.zeros((PAD, 128), F32)

    def products(table, own, size):
        below, above = one, one
        for k in range(size):
            below *= jnp.where(own > k, table[k], one)
            above *= jnp.where(own < k, table[k], one)
        return below, above

    shifted, stride, rate = steps(logit_ref[...], bias_ref[...], decay_ref[...])
    upper = (iota((LEN, LEN), 0) <= iota((LEN, LEN), 1)).astype(F32)
    total = jnp.dot(stride * rate, upper, precision=EXACT, preferred_element_type=F32)
    last = total[:, LEN - 1 : LEN]

    start = lax.axis_index("ctx") * LEN
    seg_row = jnp.zeros((1, LEN), jnp.int32)
    seg_col = jnp.zeros((LEN, 128), jnp.int32)
    entry = jnp.int32(0)
    final = jnp.int32(0)
    for d in range(docs_ref.shape[1]):
        doc = docs_ref[0, d] - start
        seg_row += (doc <= iota((1, LEN), 1)).astype(jnp.int32)
        seg_col += (doc <= iota((LEN, 128), 0)).astype(jnp.int32)
        entry += (doc <= -1).astype(jnp.int32)
        final += (doc <= LEN - 1).astype(jnp.int32)
    linked = (final == entry).astype(F32)
    lam_ref[...] = pair_rows(jnp.exp(last) * linked)

    pl.semaphore_wait(barrier, len(peers))
    gather_start(zlam, z, lam_ref[...], peers[:7], 0)

    seg_col = seg_col[:, 0:1]
    same = seg_col == seg_row
    mask[...] = jnp.where(same & (iota((LEN, LEN), 0) >= iota((LEN, LEN), 1)), 0.0, NEG)
    mask_t[...] = jnp.where(same & (iota((LEN, LEN), 0) <= iota((LEN, LEN), 1)), 0.0, NEG)
    keep = (seg_row == entry).astype(F32)
    own = (seg_row == final).astype(F32)
    moved = total - jnp.log(stride)
    row_l[...] = total
    row_m[...] = moved
    stack_w[...] = stacked(own * jnp.exp(last - total) * stride)
    stack_f[...] = stacked(keep * jnp.exp(total))
    stack_l[...] = stacked(total)
    stack_m[...] = stacked(moved)
    b = b_ref[...]
    c = c_ref[...]
    gram[...] = mm_nt(c, b)
    gram_t[...] = mm_nt(b, c)
    b_t[...] = b.astype(F32).T.astype(BF16)
    c_t[...] = c.astype(F32).T.astype(BF16)
    dg_ref[...] = jnp.zeros((LEN, LEN), F32)
    gains[...] = pair_rows(to_column(skip_ref[...]))
    db[...] = jnp.zeros_like(db)
    dc[...] = jnp.zeros_like(dc)
    row_last[...] = jnp.zeros_like(row_last)
    row_skip[...] = jnp.zeros_like(row_skip)

    @pl.when(z == 0)
    def _():
        up_in[...] = jnp.zeros_like(up_in)

    @pl.when(z == NZ - 1)
    def _():
        down_in[...] = jnp.zeros_like(down_in)

    gather_end(zlam, z, NZ, peers[:7], 0)
    below_z, above_z = products(zlam, z, NZ)
    coef[0, 0] = lam_ref[...]
    coef[1, 0] = lam_ref[...]
    coef[0, 1] = above_z
    coef[1, 1] = below_z
    gather_start(xlam, x, below_z * above_z * lam_ref[...], peers[7:10], 7)

    def gather_mid():
        gather_end(xlam, x, NX, peers[7:10], 7)
        below_x, above_x = products(xlam, x, NX)
        gather_start(ylam, y, below_x * above_x * xlam[x], peers[10:13], 10)

    def ring_of_four(table, own):
        mine, other = table[own], table[partner(own)]
        both = mine * other
        across = table[3 - own] * table[partner(3 - own)]
        odd = own % 2 == 1
        upper = own >= 2
        forward = (
            jnp.where(odd, one, other),
            jnp.where(odd, mine, one),
            jnp.where(odd, one, zero),
            jnp.where(upper, one, across),
            jnp.where(upper, both, one),
            jnp.where(upper, jnp.where(odd, other, one), zero),
        )
        backward = (
            jnp.where(odd, other, one),
            jnp.where(odd, one, mine),
            jnp.where(odd, zero, one),
            jnp.where(upper, across, one),
            jnp.where(upper, one, both),
            jnp.where(upper, zero, jnp.where(odd, one, other)),
        )
        return forward, backward

    def gather_last():
        gather_end(ylam, y, NY, peers[10:13], 10)
        below_x, above_x = products(xlam, x, NX)
        in_x = ring_of_four(xlam, x)
        in_y = ring_of_four(ylam, y)
        for d in range(2):
            outer = coef[1 - d, 1]
            outer_x = outer * (below_x if d == 0 else above_x)
            table = (
                in_x[d][0],
                in_x[d][1],
                in_x[d][3],
                in_x[d][4],
                in_y[d][0],
                in_y[d][1],
                outer * in_x[d][2],
                outer * in_x[d][5],
                outer_x * in_y[d][2],
                outer_x * in_y[d][5],
            )
            for k, value in enumerate(table):
                coef[d, k + 2] = value

    to_up = at(y, x, (z + 1) % NZ)
    to_down = at(y, x, (z + NZ - 1) % NZ)
    to_x1 = at(y, partner(x), z)
    to_x2 = at(y, 3 - x, z)
    to_y1 = at(partner(y), x, z)
    to_y2 = at(3 - y, x, z)

    def link(stage, c, source, target, device):
        return pltpu.make_async_remote_copy(
            src_ref=source.at[c],
            dst_ref=target.at[c],
            send_sem=send_sem.at[stage, c],
            recv_sem=recv_sem.at[stage, c],
            device_id=device,
            device_id_type=MESH,
        )

    links = (
        functools.partial(link, 0, source=up_out, target=up_in, device=to_up),
        functools.partial(link, 1, source=down_out, target=down_in, device=to_down),
        functools.partial(link, 2, source=t_out, target=x1_in, device=to_x1),
        functools.partial(link, 3, source=u2_out, target=x2_in, device=to_x2),
        functools.partial(link, 4, source=u_out, target=y1_in, device=to_y1),
        functools.partial(link, 5, source=v2_out, target=y2_in, device=to_y2),
    )

    def staged(c):
        return (c >= 0) & (c < CHUNKS)

    lag_t = HOP * jnp.maximum(z, NZ - 1 - z)
    first = iota((LEN, 128), 1) < HALF

    def row(d, k, c):
        return coef[d, k, pl.ds(c // SPLIT, 1), :]

    def begin_pair(j):
        lanes = pl.ds(pl.multiple_of(j * 128, 128), 128)
        expand = spread(j)
        w = mm(stack_w[...], expand)
        f = mm(stack_f[...], expand)
        wide_w[:, lanes] = w
        wide_f[:, lanes] = f
        high, low = split2(w * x_ref[:, lanes].astype(F32))
        state = mm(b_t[...], high) + mm(b_t[...], low)
        high, low = split2(f * dy_ref[:, lanes].astype(F32))
        state_b = mm(c_t[...], high) + mm(c_t[...], low)
        for k in range(SPLIT):
            state_ref[SPLIT * j + k, 0] = state[k * ROWS : (k + 1) * ROWS]
            state_ref[SPLIT * j + k, 1] = state_b[k * ROWS : (k + 1) * ROWS]

    def mix_head(h):
        j = h // 2
        second = h % 2 == 1
        lanes = pl.ds(pl.multiple_of(j * 128, 128), 128)
        xs = x_ref[:, lanes]
        dys = dy_ref[:, lanes]
        expand = spread(j)
        columns_l = mm(stack_l[...], expand)
        columns_m = mm(stack_m[...], expand)
        lrow = row_l[pl.ds(h, 1), :]
        mrow = row_m[pl.ds(h, 1), :]
        lcol = jnp.where(second, columns_l[:, HALF : HALF + 1], columns_l[:, 0:1])
        mcol = jnp.where(second, columns_m[:, HALF : HALF + 1], columns_m[:, 0:1])
        ours = first != second
        decays = jnp.exp((lcol - mrow) + mask[...])
        high, low = split2(decays * gram[...])
        y_ref[:, lanes] = jnp.where(ours, mm(high, xs) + mm(low, xs), y_ref[:, lanes])
        part = jnp.where(ours, dys, jnp.zeros_like(dys))
        dg_ref[...] += mm_nt(part, xs) * decays
        decays_t = jnp.exp((lrow - mcol) + mask_t[...])
        high, low = split2(decays_t * gram_t[...])
        dx_ref[:, lanes] = jnp.where(ours, mm(high, dys) + mm(low, dys), dx_ref[:, lanes])

    def finish_pair(j):
        lanes = pl.ds(pl.multiple_of(j * 128, 128), 128)
        both = []
        for d, near in ((0, up_in), (1, down_in)):
            pieces = []
            for k in range(SPLIT):
                c_end = SPLIT * j + k
                pieces.append(
                    near[c_end, d]
                    + (
                        (row(d, 8, c_end) * x1_in[c_end, d] + row(d, 9, c_end) * x2_in[c_end, d])
                        + (row(d, 10, c_end) * y1_in[c_end, d] + row(d, 11, c_end) * y2_in[c_end, d])
                    )
                )
            both.append(jnp.concatenate(pieces, axis=0))
        state_in, adjoint = both
        state_end = jnp.concatenate([state_ref[SPLIT * j + k, 0] for k in range(SPLIT)], axis=0)
        xs = x_ref[:, lanes].astype(F32)
        dys = dy_ref[:, lanes].astype(F32)
        w = wide_w[:, lanes]
        f = wide_f[:, lanes]
        gain = gains[pl.ds(j, 1), :]
        s_high, s_low = split2(state_in)
        a_high, a_low = split2(adjoint)
        inner = y_ref[:, lanes] + f * (mm(c_ref[...], s_high) + mm(c_ref[...], s_low))
        inner_t = dx_ref[:, lanes] + w * (mm(b_ref[...], a_high) + mm(b_ref[...], a_low))
        mixed_ref[:, lanes] = (inner + gain * xs).astype(BF16)
        feature_ref[:, lanes] = (inner_t + gain * dys).astype(BF16)
        select = (iota((8, 128), 1) // HALF == iota((8, 128), 0)).astype(BF16)
        high, middle, low = split3(dys * inner)
        r = mm_nt(select, high) + (mm_nt(select, middle) + mm_nt(select, low))
        high, middle, low = split3(xs * inner_t)
        v = mm_nt(select, high) + (mm_nt(select, middle) + mm_nt(select, low))
        for k in range(2):
            rows_r[pl.ds(2 * j + k, 1), :] = r[k : k + 1]
            rows_v[pl.ds(2 * j + k, 1), :] = v[k : k + 1]
        high, low = split2(f * dys)
        dc[...] += mm_nt(high, s_high) + (mm_nt(high, s_low) + mm_nt(low, s_high))
        high, low = split2(w * xs)
        db[...] += mm_nt(high, a_high) + (mm_nt(high, a_low) + mm_nt(low, a_high))
        row_skip[pl.ds(j, 1), :] = jnp.sum(dys * xs, axis=0, keepdims=True)
        leaving = lam_ref[pl.ds(j, 1), :] * state_in + state_end
        row_last[pl.ds(j, 1), :] = jnp.sum(adjoint * leaving, axis=0, keepdims=True)

    def tick(i, carry):
        @pl.when((i < CHUNKS) & (i % SPLIT == 0))
        def _():
            begin_pair(i // SPLIT)

        c_up = i - HOP * z

        @pl.when(staged(c_up))
        def _():
            @pl.when(z > 0)
            def _():
                links[0](c_up).wait_recv()

            up_out[c_up, 0] = row(0, 0, c_up) * up_in[c_up, 0] + state_ref[c_up, 0]
            up_out[c_up, 1] = up_in[c_up, 1] + row(1, 1, c_up) * state_ref[c_up, 1]

            @pl.when(z < NZ - 1)
            def _():
                links[0](c_up).start()

        c_down = i - HOP * (NZ - 1 - z)

        @pl.when(staged(c_down))
        def _():
            @pl.when(z < NZ - 1)
            def _():
                links[1](c_down).wait_recv()

            down_out[c_down, 0] = down_in[c_down, 0] + row(0, 1, c_down) * state_ref[c_down, 0]
            down_out[c_down, 1] = row(1, 0, c_down) * down_in[c_down, 1] + state_ref[c_down, 1]

            @pl.when(z > 0)
            def _():
                links[1](c_down).start()

        @pl.when(i == GATHER_X)
        def _():
            gather_mid()

        @pl.when(i == GATHER_Y)
        def _():
            gather_last()

        c_t = i - lag_t

        @pl.when(staged(c_t))
        def _():
            t_out[c_t, 0] = up_out[c_t, 0] * row(0, 1, c_t) + down_in[c_t, 0]
            t_out[c_t, 1] = down_out[c_t, 1] * row(1, 1, c_t) + up_in[c_t, 1]
            links[2](c_t).start()

        for stage, mine, came, result, k in (
            (2, t_out, x1_in, u2_out, 2),
            (3, u2_out, x2_in, u_out, 4),
            (4, u_out, y1_in, v2_out, 6),
        ):
            c = c_t - HOP * (stage - 1)

            @pl.when(staged(c))
            def _(stage=stage, mine=mine, came=came, result=result, k=k, c=c):
                links[stage](c).wait_recv()
                for d in range(2):
                    result[c, d] = row(d, k, c) * mine[c, d] + row(d, k + 1, c) * came[c, d]
                links[stage + 1](c).start()

        @pl.when(i < HEADS)
        def _():
            mix_head(i)

        c_end = c_t - HOP * 4

        @pl.when(staged(c_end) & (c_end % SPLIT == SPLIT - 1))
        def _():
            for k in range(SPLIT):
                links[5](c_end - (SPLIT - 1 - k)).wait_recv()
            finish_pair(c_end // SPLIT)

        return carry

    lax.fori_loop(0, CHUNKS + HOP * (NZ - 1 + 4), tick, 0)

    dg = dg_ref[...]
    high, low = split2(dg)
    read_ref[...] = (dc[...] + (mm(high, b_ref[...]) + mm(low, b_ref[...]))).astype(BF16)
    high, low = split2(dg.T)
    write_ref[...] = (db[...] + (mm(high, c_ref[...]) + mm(low, c_ref[...]))).astype(BF16)

    shifted, stride, rate = steps(logit_ref[...], bias_ref[...], decay_ref[...])
    v = rows_v[...]
    is_last = iota((HEADS, LEN), 1) == LEN - 1
    slope = rows_r[...] - v + jnp.where(is_last, unpair_sums(row_last[...]), 0.0)
    lower = (iota((LEN, LEN), 0) >= iota((LEN, LEN), 1)).astype(F32)
    slope = jnp.dot(slope, lower, precision=EXACT, preferred_element_type=F32)
    step = (v / stride + rate * slope) * (1.0 / (1.0 + jnp.exp(-shifted)))
    step_ref[...] = step
    bias_sum = jnp.sum(step, axis=1, keepdims=True)
    decay_sum = jnp.sum(slope * (rate * stride), axis=1, keepdims=True)
    skip_sum = unpair_sums(row_skip[...])
    sums = jnp.concatenate(
        [to_row(bias_sum), to_row(decay_sum), to_row(skip_sum), jnp.zeros((5, 128), F32)], axis=0
    )
    gather_start(csum, core, sums, peers[13:14], 13)
    gather_end(csum, core, 2, peers[13:14], 13)
    gather_start(zsum, z, csum[0] + csum[1], peers[:7], 14)
    gather_end(zsum, z, NZ, peers[:7], 14)
    gather_start(xsum, x, jnp.sum(zsum[...], axis=0), peers[7:10], 21)
    gather_end(xsum, x, NX, peers[7:10], 21)
    gather_start(ysum, y, jnp.sum(xsum[...], axis=0), peers[10:13], 24)
    gather_end(ysum, y, NY, peers[10:13], 24)
    sums = jnp.sum(ysum[...], axis=0)
    bias_out[...] = sums[0:1, :HEADS]
    decay_out[...] = sums[1:2, :HEADS]
    skip_out[...] = sums[2:3, :HEADS]

    def drain(c, carry):
        @pl.when(z < NZ - 1)
        def _():
            links[0](c).wait_send()

        @pl.when(z > 0)
        def _():
            links[1](c).wait_send()

        for stage in range(2, 6):
            links[stage](c).wait_send()
        return carry

    lax.fori_loop(0, CHUNKS, drain, 0)


VM = pl.BlockSpec(memory_space=pltpu.VMEM)
SM = pl.BlockSpec(memory_space=pltpu.SMEM)


def shape(dims, kind=F32):
    return jax.ShapeDtypeStruct(dims, kind)


def local(
    features,
    write_keys,
    read_queries,
    step_logits,
    step_bias,
    decay_log,
    skip_gain,
    doc_starts,
    out_grad,
):
    x, b, c, logits, dy = features[0], write_keys[0], read_queries[0], step_logits[0], out_grad[0]
    bias, decay, skip = step_bias[None], decay_log[None], skip_gain[None]
    carry_shape = (CHUNKS, 2, ROWS, 128)
    outputs = pl.pallas_call(
        layer_kernel,
        out_shape=(
            shape((LEN, WIDE), BF16),
            shape((LEN, WIDE), BF16),
            shape((LEN, 128), BF16),
            shape((LEN, 128), BF16),
            shape((HEADS, LEN)),
            shape((1, HEADS)),
            shape((1, HEADS)),
            shape((1, HEADS)),
        ),
        in_specs=[SM] + [VM] * 8,
        out_specs=(VM,) * 8,
        scratch_shapes=[pltpu.VMEM(carry_shape, F32)] * 13
        + [pltpu.VMEM((n, PAD, 128), F32) for n in (NZ, NX, NY)]
        + [pltpu.VMEM((2, 12, PAD, 128), F32)]
        + [pltpu.VMEM((n, 8, 128), F32) for n in (NZ, NX, NY, 2)]
        + [pltpu.VMEM((LEN, WIDE), F32)] * 4
        + [pltpu.VMEM((LEN, LEN), F32)]
        + [pltpu.VMEM((LEN, 128), BF16)] * 4
        + [pltpu.VMEM((HEADS, LEN), F32)] * 2
        + [pltpu.VMEM((LEN, LEN), F32)] * 4
        + [pltpu.VMEM((128, LEN), BF16)] * 2
        + [pltpu.VMEM((LEN, 128), F32)] * 2
        + [pltpu.VMEM((HEADS, LEN), F32)] * 2
        + [pltpu.VMEM((PAD, 128), F32)] * 4
        + [pltpu.SemaphoreType.DMA((6, CHUNKS))] * 2
        + [pltpu.SemaphoreType.DMA((27,))] * 2,
        compiler_params=pltpu.CompilerParams(
            collective_id=0, has_side_effects=True, vmem_limit_bytes=60 * 2**20
        ),
        name="layer",
    )(doc_starts, x, dy, b, c, logits, bias, decay, skip)
    mixed, feature_grad, write_grad, read_grad, step_grad, bias_sum, decay_sum, skip_sum = outputs
    return (
        mixed[None],
        feature_grad[None],
        write_grad[None],
        read_grad[None],
        step_grad[None],
        bias_sum[0],
        decay_sum[0],
        skip_sum[0],
    )


def solution(mesh):
    in_specs = (
        P("dp", "ctx", None),
        P("dp", "ctx", None),
        P("dp", "ctx", None),
        P("dp", None, "ctx"),
        P(),
        P(),
        P(),
        P("dp", None),
        P("dp", "ctx", None),
    )
    out_specs = (
        P("dp", "ctx", None),
        P("dp", "ctx", None),
        P("dp", "ctx", None),
        P("dp", "ctx", None),
        P("dp", None, "ctx"),
        P(),
        P(),
        P(),
    )
    return jax.shard_map(local, mesh=mesh, in_specs=in_specs, out_specs=out_specs, check_vma=False)
```

time: 265 us -> 145 us (0.55)
  blocking collectives: 94.4 us -> 0 us
  Pallas kernels: 169 us -> 137 us
  local copies, waits for them, and re-layouts: 0.52 us -> 7.06 us
    psum x1 -> x0, blocking collectives: 94.4 us -> none  [local(): sums = lax.psum(sums, ('dp', 'ctx'))]
    pallas_call x3 -> x1, Pallas kernels: 169 us -> 137 us  [local(): pl.pallas_call(layer_kernel, out_shape=(shape((LEN, WIDE), BF16), shape((...]
    unnamed x0 -> x22, local copies, waits for them, and re-layouts: none -> 7.06 us
where the time goes in v2:
time: 145 us; the launch traced here: 144 us
  Pallas kernels  137 us (94%)
  local copies, waits for them, and re-layouts  7.06 us (5%)
    pallas_call x1, Pallas kernels, local(): pl.pallas_call(layer_kernel, out_shape=(shape((LEN, WIDE), BF16), shape((...  137 us
    unnamed x22, local copies, waits for them, and re-layouts  7.06 us

profile of v2, /device:TPU:1, one launch (start us, length us, event | category | flops | bytes accessed | tf_op | source)
XLA Modules:
  0.0 144.4 jit_solution(16037228308581355100)
XLA Ops:
  0.6 136.7 %layer.1 = (bf16[256,2560]{1,0:T(8,128)(2,1)}, bf16[256,2560]{1,0:T(8,128)(2,1)}, bf16[256,128]{1,0:T(8,128)(2,1)}, bf16[256,128]{1,0:T(8,128)(2,1)}, f32[40,256...) custom-call(s32[1,32]{1,0:T(1,128)} %docs_ref.1, bf16[256,2560]{1,0:T(8,128)(2,1)} %bitcast.16, ...), custom_call_target="tpu_custom_call" | custom-call | tf_op jit(solution)/shard_map/layer/pallas_call | solution.py:619
  137.3 0.0 copy-start
  137.4 2.6 %copy.25 = bf16[1,256,2560]{2,1,0:T(8,128)(2,1)} copy(bf16[1,256,2560]{2,1,0:T(8,128)(2,1)} %bitcast.19) | data formatting | bytes 2621440
  139.9 0.0 copy-done
  139.9 0.0 copy-start.2
  139.9 0.0 copy-start.1
  139.9 0.0 copy-start.3
  139.9 0.0 copy-start.6
  139.9 0.0 copy-start.5
  139.9 0.0 copy-start.4
  140.0 1.1 copy.26
  141.0 0.0 copy-done.2
  141.0 0.6 copy.27
  141.6 0.0 copy-done.1
  141.7 0.6 copy.28
  142.3 0.0 copy-done.3
  142.3 0.6 copy.29
  142.9 0.0 copy-done.6
  142.9 0.5 copy.30
  143.4 0.0 copy-done.5
  143.4 0.5 copy.31
  143.9 0.0 copy-done.4
  143.9 0.5 copy.32
Async XLA Ops:
  137.3 2.6 %copy-start = (bf16[256,2560]{1,0:T(8,128)(2,1)S(1)}, bf16[256,2560]{1,0:T(8,128)(2,1)}, u32[]{:S(2)}) copy-start(bf16[256,2560]{1,0:T(8,128)(2,1)} %get-tuple-element.17) | copy-start | bytes 3932164
  139.9 1.1 copy-start.2
  139.9 1.7 %copy-start.1 = (bf16[256,128]{1,0:T(8,128)(2,1)S(1)}, bf16[256,128]{1,0:T(8,128)(2,1)}, u32[]{:S(2)}) copy-start(bf16[256,128]{1,0:T(8,128)(2,1)} %get-tuple-element.19) | copy-start | bytes 196612
  139.9 2.4 %copy-start.3 = (f32[40,256]{1,0:T(8,128)S(1)}, f32[40,256]{1,0:T(8,128)}, u32[]{:S(2)}) copy-start(f32[40,256]{1,0:T(8,128)} %get-tuple-element.20) | copy-start | bytes 122884
  139.9 3.0 %copy-start.6 = (f32[1,40]{1,0:T(1,128)S(1)}, f32[1,40]{1,0:T(1,128)}, u32[]{:S(2)}) copy-start(f32[1,40]{1,0:T(1,128)} %get-tuple-element.21) | copy-start | bytes 484
  139.9 3.5 %copy-start.5 = (f32[1,40]{1,0:T(1,128)S(1)}, f32[1,40]{1,0:T(1,128)}, u32[]{:S(2)}) copy-start(f32[1,40]{1,0:T(1,128)} %get-tuple-element.22) | copy-start | bytes 484
  139.9 4.0 %copy-start.4 = (f32[1,40]{1,0:T(1,128)S(1)}, f32[1,40]{1,0:T(1,128)}, u32[]{:S(2)}) copy-start(f32[1,40]{1,0:T(1,128)} %get-tuple-element.23) | copy-start | bytes 484

commit v3 on v2

--- a/solution.py
+++ b/solution.py
@@ -23,8 +23,11 @@
 ROWS = 128 // SPLIT
 NY, NX, NZ = 4, 4, 8
 HOP = 3
-GATHER_X = 3
-GATHER_Y = 7
+GATHER_Z = HOP - 1
+GATHER_X = 2 * HOP - 1
+GATHER_Y = 3 * HOP - 1
+LATER = HOP
+SET = CHUNKS // 2
 NEG = -1e30
 
 
@@ -152,14 +155,14 @@
     y1_in,
     v2_out,
     y2_in,
+    f_buf,
+    entering,
     zlam,
     xlam,
     ylam,
     coef,
-    zsum,
-    xsum,
-    ysum,
-    csum,
+    column_sums,
+    plane_sums,
     wide_w,
     wide_f,
     y_ref,
@@ -193,10 +196,20 @@
     y, x, z = place()
     core = lax.axis_index("dp")
     barrier = pltpu.get_barrier_semaphore()
-    peers = [at(y, x, (z + k) % NZ) for k in range(1, NZ)]
-    peers += [at(y, (x + k) % NX, z) for k in range(1, NX)]
-    peers += [at((y + k) % NY, x, z) for k in range(1, NY)]
-    peers += [(1 - core, lax.axis_index("ctx"))]
+    along_z = [at(y, x, (z + k) % NZ) for k in range(1, NZ)]
+    along_x = [at(y, (x + k) % NX, z) for k in range(1, NX)]
+    along_y = [at((y + k) % NY, x, z) for k in range(1, NY)]
+    column = core * NZ + z
+    cell = y * NX + x
+    in_column = []
+    for k in range(1, 2 * NZ):
+        other = (column + k) % (2 * NZ)
+        in_column.append((other // NZ, cell * NZ + other % NZ))
+    in_plane = []
+    for k in range(1, NX * NY):
+        other = (cell + k) % (NX * NY)
+        in_plane.append((core, other * NZ + z))
+    peers = in_column + in_plane
     for peer in peers:
         pl.semaphore_signal(barrier, inc=1, device_id=peer, device_id_type=MESH)
 
@@ -251,7 +264,7 @@
     lam_ref[...] = pair_rows(jnp.exp(last) * linked)
 
     pl.semaphore_wait(barrier, len(peers))
-    gather_start(zlam, z, lam_ref[...], peers[:7], 0)
+    gather_start(zlam, z, lam_ref[...], along_z, 0)
 
     seg_col = seg_col[:, 0:1]
     same = seg_col == seg_row
@@ -287,18 +300,16 @@
     def _():
         down_in[...] = jnp.zeros_like(down_in)
 
-    gather_end(zlam, z, NZ, peers[:7], 0)
-    below_z, above_z = products(zlam, z, NZ)
-    coef[0, 0] = lam_ref[...]
-    coef[1, 0] = lam_ref[...]
-    coef[0, 1] = above_z
-    coef[1, 1] = below_z
-    gather_start(xlam, x, below_z * above_z * lam_ref[...], peers[7:10], 7)
-
-    def gather_mid():
-        gather_end(xlam, x, NX, peers[7:10], 7)
-        below_x, above_x = products(xlam, x, NX)
-        gather_start(ylam, y, below_x * above_x * xlam[x], peers[10:13], 10)
+    for d in range(2):
+        coef[d, 0] = lam_ref[...]
+        coef[d, 1] = one
+
+    def gather_first():
+        gather_end(zlam, z, NZ, along_z, 0)
+        below_z, above_z = products(zlam, z, NZ)
+        coef[0, 1] = above_z
+        coef[1, 1] = below_z
+        gather_start(xlam, x, below_z * above_z * lam_ref[...], along_x, 7)
 
     def ring_of_four(table, own):
         mine, other = table[own], table[partner(own)]
@@ -324,28 +335,28 @@
         )
         return forward, backward
 
+    def put(d, k, values):
+        for value in values:
+            coef[d, k] = value
+            k += 1
+
+    def gather_mid():
+        gather_end(xlam, x, NX, along_x, 7)
+        below_x, above_x = products(xlam, x, NX)
+        gather_start(ylam, y, below_x * above_x * xlam[x], along_y, 10)
+        in_x = ring_of_four(xlam, x)
+        for d in range(2):
+            put(d, 2, (in_x[d][0], in_x[d][1], in_x[d][3], in_x[d][4]))
+            put(d, 8, (in_x[d][2], in_x[d][5]))
+
     def gather_last():
-        gather_end(ylam, y, NY, peers[10:13], 10)
+        gather_end(ylam, y, NY, along_y, 10)
         below_x, above_x = products(xlam, x, NX)
-        in_x = ring_of_four(xlam, x)
         in_y = ring_of_four(ylam, y)
         for d in range(2):
-            outer = coef[1 - d, 1]
-            outer_x = outer * (below_x if d == 0 else above_x)
-            table = (
-                in_x[d][0],
-                in_x[d][1],
-                in_x[d][3],
-                in_x[d][4],
-                in_y[d][0],
-                in_y[d][1],
-                outer * in_x[d][2],
-                outer * in_x[d][5],
-                outer_x * in_y[d][2],
-                outer_x * in_y[d][5],
-            )
-            for k, value in enumerate(table):
-                coef[d, k + 2] = value
+            outer_x = below_x if d == 0 else above_x
+            put(d, 6, (in_y[d][0], in_y[d][1]))
+            put(d, 10, (outer_x * in_y[d][2], outer_x * in_y[d][5]))
 
     to_up = at(y, x, (z + 1) % NZ)
     to_down = at(y, x, (z + NZ - 1) % NZ)
@@ -373,8 +384,16 @@
         functools.partial(link, 5, source=v2_out, target=y2_in, device=to_y2),
     )
 
-    def staged(c):
-        return (c >= 0) & (c < CHUNKS)
+    def staged(n):
+        return (n >= 0) & (n < SET)
+
+    def chunk(n, second):
+        return 4 * (n // 2) + n % 2 + 2 * second
+
+    def outside(c, d):
+        return (row(d, 8, c) * x1_in[c, d] + row(d, 9, c) * x2_in[c, d]) + (
+            row(d, 10, c) * y1_in[c, d] + row(d, 11, c) * y2_in[c, d]
+        )
 
     lag_t = HOP * jnp.maximum(z, NZ - 1 - z)
     first = iota((LEN, 128), 1) < HALF
@@ -422,20 +441,7 @@
 
     def finish_pair(j):
         lanes = pl.ds(pl.multiple_of(j * 128, 128), 128)
-        both = []
-        for d, near in ((0, up_in), (1, down_in)):
-            pieces = []
-            for k in range(SPLIT):
-                c_end = SPLIT * j + k
-                pieces.append(
-                    near[c_end, d]
-                    + (
-                        (row(d, 8, c_end) * x1_in[c_end, d] + row(d, 9, c_end) * x2_in[c_end, d])
-                        + (row(d, 10, c_end) * y1_in[c_end, d] + row(d, 11, c_end) * y2_in[c_end, d])
-                    )
-                )
-            both.append(jnp.concatenate(pieces, axis=0))
-        state_in, adjoint = both
+        state_in, adjoint = entering[0], entering[1]
         state_end = jnp.concatenate([state_ref[SPLIT * j + k, 0] for k in range(SPLIT)], axis=0)
         xs = x_ref[:, lanes].astype(F32)
         dys = dy_ref[:, lanes].astype(F32)
@@ -465,39 +471,9 @@
         row_last[pl.ds(j, 1), :] = jnp.sum(adjoint * leaving, axis=0, keepdims=True)
 
     def tick(i, carry):
-        @pl.when((i < CHUNKS) & (i % SPLIT == 0))
+        @pl.when(i == GATHER_Z)
         def _():
-            begin_pair(i // SPLIT)
-
-        c_up = i - HOP * z
-
-        @pl.when(staged(c_up))
-        def _():
-            @pl.when(z > 0)
-            def _():
-                links[0](c_up).wait_recv()
-
-            up_out[c_up, 0] = row(0, 0, c_up) * up_in[c_up, 0] + state_ref[c_up, 0]
-            up_out[c_up, 1] = up_in[c_up, 1] + row(1, 1, c_up) * state_ref[c_up, 1]
-
-            @pl.when(z < NZ - 1)
-            def _():
-                links[0](c_up).start()
-
-        c_down = i - HOP * (NZ - 1 - z)
-
-        @pl.when(staged(c_down))
-        def _():
-            @pl.when(z < NZ - 1)
-            def _():
-                links[1](c_down).wait_recv()
-
-            down_out[c_down, 0] = down_in[c_down, 0] + row(0, 1, c_down) * state_ref[c_down, 0]
-            down_out[c_down, 1] = row(1, 0, c_down) * down_in[c_down, 1] + state_ref[c_down, 1]
-
-            @pl.when(z > 0)
-            def _():
-                links[1](c_down).start()
+            gather_first()
 
         @pl.when(i == GATHER_X)
         def _():
@@ -507,43 +483,129 @@
         def _():
             gather_last()
 
-        c_t = i - lag_t
-
-        @pl.when(staged(c_t))
+        @pl.when(i < PAIRS)
         def _():
-            t_out[c_t, 0] = up_out[c_t, 0] * row(0, 1, c_t) + down_in[c_t, 0]
-            t_out[c_t, 1] = down_out[c_t, 1] * row(1, 1, c_t) + up_in[c_t, 1]
-            links[2](c_t).start()
-
-        for stage, mine, came, result, k in (
-            (2, t_out, x1_in, u2_out, 2),
-            (3, u2_out, x2_in, u_out, 4),
-            (4, u_out, y1_in, v2_out, 6),
-        ):
-            c = c_t - HOP * (stage - 1)
-
-            @pl.when(staged(c))
-            def _(stage=stage, mine=mine, came=came, result=result, k=k, c=c):
-                links[stage](c).wait_recv()
+            begin_pair(i)
+
+        def chains(second):
+            since = i - (LATER + 4 * HOP) * second
+            n = since - HOP * z
+
+            @pl.when(staged(n))
+            def _(second=second, n=n):
+                c = chunk(n, second)
+
+                @pl.when(z > 0)
+                def _():
+                    links[0](c).wait_recv()
+
+                if second:
+                    ahead = up_in[c, 0] + row(1, 1, c) * f_buf[c, 0]
+                    up_out[c, 0] = row(0, 0, c) * ahead + state_ref[c, 0]
+                    up_out[c, 1] = up_in[c, 1] + f_buf[c, 1]
+                else:
+                    up_out[c, 0] = row(0, 0, c) * up_in[c, 0] + state_ref[c, 0]
+                    up_out[c, 1] = up_in[c, 1] + row(1, 1, c) * state_ref[c, 1]
+
+                @pl.when(z < NZ - 1)
+                def _():
+                    links[0](c).start()
+
+            n = since - HOP * (NZ - 1 - z)
+
+            @pl.when(staged(n))
+            def _(second=second, n=n):
+                c = chunk(n, second)
+
+                @pl.when(z < NZ - 1)
+                def _():
+                    links[1](c).wait_recv()
+
+                if second:
+                    ahead = down_in[c, 1] + row(0, 1, c) * f_buf[c, 1]
+                    down_out[c, 0] = down_in[c, 0] + f_buf[c, 0]
+                    down_out[c, 1] = row(1, 0, c) * ahead + state_ref[c, 1]
+                else:
+                    down_out[c, 0] = down_in[c, 0] + row(0, 1, c) * state_ref[c, 0]
+                    down_out[c, 1] = row(1, 0, c) * down_in[c, 1] + state_ref[c, 1]
+
+                @pl.when(z > 0)
+                def _():
+                    links[1](c).start()
+
+        def exchanges(second):
+            first_at = i - LATER if second else i - lag_t
+
+            @pl.when(staged(first_at))
+            def _(second=second, first_at=first_at):
+                c = chunk(first_at, second)
+                if second:
+                    t_out[c, 0] = row(0, 1, c) * state_ref[c, 0]
+                    t_out[c, 1] = row(1, 1, c) * state_ref[c, 1]
+                else:
+                    t_out[c, 0] = up_out[c, 0] * row(0, 1, c) + down_in[c, 0]
+                    t_out[c, 1] = down_out[c, 1] * row(1, 1, c) + up_in[c, 1]
+                links[2](c).start()
+
+            for stage, mine, came, result, k in (
+                (2, t_out, x1_in, u2_out, 2),
+                (3, u2_out, x2_in, u_out, 4),
+                (4, u_out, y1_in, v2_out, 6),
+            ):
+                n = first_at - HOP * (stage - 1)
+
+                @pl.when(staged(n))
+                def _(stage=stage, mine=mine, came=came, result=result, k=k, n=n, second=second):
+                    c = chunk(n, second)
+                    links[stage](c).wait_recv()
+                    for d in range(2):
+                        result[c, d] = row(d, k, c) * mine[c, d] + row(d, k + 1, c) * came[c, d]
+                    links[stage + 1](c).start()
+
+            n = first_at - HOP * 4
+
+            @pl.when(staged(n))
+            def _(second=second, n=n):
+                c = chunk(n, second)
+                links[5](c).wait_recv()
                 for d in range(2):
-                    result[c, d] = row(d, k, c) * mine[c, d] + row(d, k + 1, c) * came[c, d]
-                links[stage + 1](c).start()
+                    f_buf[c, d] = outside(c, d)
+
+        exchanges(1)
+        chains(0)
+        chains(1)
+        exchanges(0)
 
         @pl.when(i < HEADS)
         def _():
             mix_head(i)
 
-        c_end = c_t - HOP * 4
-
-        @pl.when(staged(c_end) & (c_end % SPLIT == SPLIT - 1))
+        for second in (0, 1):
+            n = i - lag_t - HOP * 4 - LATER * second
+
+            @pl.when(staged(n) & (n % 2 == 1))
+            def _(second=second, n=n):
+                for k in range(2):
+                    c = chunk(n - 1 + k, second)
+                    lines = slice(k * ROWS, (k + 1) * ROWS)
+                    if second:
+                        entering[0, lines] = up_in[c, 0] + row(1, 1, c) * (down_in[c, 0] + f_buf[c, 0])
+                        entering[1, lines] = down_in[c, 1] + row(0, 1, c) * (up_in[c, 1] + f_buf[c, 1])
+                    else:
+                        entering[0, lines] = up_in[c, 0] + row(1, 1, c) * f_buf[c, 0]
+                        entering[1, lines] = down_in[c, 1] + row(0, 1, c) * f_buf[c, 1]
+
+        done_at = i - lag_t - HOP * 4
+        second = 1 - done_at % 2
+        n = done_at - LATER * second
+
+        @pl.when(staged(n))
         def _():
-            for k in range(SPLIT):
-                links[5](c_end - (SPLIT - 1 - k)).wait_recv()
-            finish_pair(c_end // SPLIT)
+            finish_pair(2 * (n // 2) + second)
 
         return carry
 
-    lax.fori_loop(0, CHUNKS + HOP * (NZ - 1 + 4), tick, 0)
+    lax.fori_loop(0, SET + HOP * (NZ - 1 + 4) + LATER, tick, 0)
 
     dg = dg_ref[...]
     high, low = split2(dg)
@@ -565,15 +627,11 @@
     sums = jnp.concatenate(
         [to_row(bias_sum), to_row(decay_sum), to_row(skip_sum), jnp.zeros((5, 128), F32)], axis=0
     )
-    gather_start(csum, core, sums, peers[13:14], 13)
-    gather_end(csum, core, 2, peers[13:14], 13)
-    gather_start(zsum, z, csum[0] + csum[1], peers[:7], 14)
-    gather_end(zsum, z, NZ, peers[:7], 14)
-    gather_start(xsum, x, jnp.sum(zsum[...], axis=0), peers[7:10], 21)
-    gather_end(xsum, x, NX, peers[7:10], 21)
-    gather_start(ysum, y, jnp.sum(xsum[...], axis=0), peers[10:13], 24)
-    gather_end(ysum, y, NY, peers[10:13], 24)
-    sums = jnp.sum(ysum[...], axis=0)
+    gather_start(column_sums, column, sums, in_column, 13)
+    gather_end(column_sums, column, 2 * NZ, in_column, 13)
+    gather_start(plane_sums, cell, jnp.sum(column_sums[...], axis=0), in_plane, 28)
+    gather_end(plane_sums, cell, NX * NY, in_plane, 28)
+    sums = jnp.sum(plane_sums[...], axis=0)
     bias_out[...] = sums[0:1, :HEADS]
     decay_out[...] = sums[1:2, :HEADS]
     skip_out[...] = sums[2:3, :HEADS]
@@ -592,6 +650,12 @@
         return carry
 
     lax.fori_loop(0, CHUNKS, drain, 0)
+
+
+def emit_kernel(*refs):
+    count = len(refs) // 2
+    for k in range(count):
+        refs[count + k][...] = refs[k][...]
 
 
 VM = pl.BlockSpec(memory_space=pltpu.VMEM)
@@ -630,10 +694,11 @@
         ),
         in_specs=[SM] + [VM] * 8,
         out_specs=(VM,) * 8,
-        scratch_shapes=[pltpu.VMEM(carry_shape, F32)] * 13
+        scratch_shapes=[pltpu.VMEM(carry_shape, F32)] * 14
+        + [pltpu.VMEM((2, 128, 128), F32)]
         + [pltpu.VMEM((n, PAD, 128), F32) for n in (NZ, NX, NY)]
         + [pltpu.VMEM((2, 12, PAD, 128), F32)]
-        + [pltpu.VMEM((n, 8, 128), F32) for n in (NZ, NX, NY, 2)]
+        + [pltpu.VMEM((n, 8, 128), F32) for n in (2 * NZ, NX * NY)]
         + [pltpu.VMEM((LEN, WIDE), F32)] * 4
         + [pltpu.VMEM((LEN, LEN), F32)]
         + [pltpu.VMEM((LEN, 128), BF16)] * 4
@@ -644,12 +709,19 @@
         + [pltpu.VMEM((HEADS, LEN), F32)] * 2
         + [pltpu.VMEM((PAD, 128), F32)] * 4
         + [pltpu.SemaphoreType.DMA((6, CHUNKS))] * 2
-        + [pltpu.SemaphoreType.DMA((27,))] * 2,
+        + [pltpu.SemaphoreType.DMA((43,))] * 2,
         compiler_params=pltpu.CompilerParams(
             collective_id=0, has_side_effects=True, vmem_limit_bytes=60 * 2**20
         ),
         name="layer",
     )(doc_starts, x, dy, b, c, logits, bias, decay, skip)
+    outputs = pl.pallas_call(
+        emit_kernel,
+        out_shape=tuple(shape(o.shape, o.dtype) for o in outputs),
+        in_specs=[VM] * 8,
+        out_specs=(VM,) * 8,
+        name="emit",
+    )(*outputs)
     mixed, feature_grad, write_grad, read_grad, step_grad, bias_sum, decay_sum, skip_sum = outputs
     return (
         mixed[None],

time: 145 us -> 136 us (0.938)
  local copies, waits for them, and re-layouts: 7.06 us -> 0 us
  Pallas kernels: 137 us -> 135 us
    unnamed x22 -> x0, local copies, waits for them, and re-layouts: 7.06 us -> none
    pallas_call x1, Pallas kernels: 137 us -> 132 us  [local(): pl.pallas_call(layer_kernel, out_shape=(shape((LEN, WIDE), BF16), shape((...]
    pallas_call x0 -> x1, Pallas kernels: none -> 3.36 us  [local(): pl.pallas_call(emit_kernel, out_shape=tuple((shape(o.shape, o.dtype) for...]
where the time goes in v3:
time: 136 us
  Pallas kernels  135 us (99%)
    pallas_call x1, Pallas kernels, local(): pl.pallas_call(layer_kernel, out_shape=(shape((LEN, WIDE), BF16), shape((...  132 us
    pallas_call x1, Pallas kernels, local(): pl.pallas_call(emit_kernel, out_shape=tuple((shape(o.shape, o.dtype) for...  3.36 us

profile of v3, /device:TPU:1, one launch (start us, length us, event | category | flops | bytes accessed | tf_op | source)
XLA Modules:
  0.0 135.9 jit_solution(2658357153393004821)
XLA Ops:
  0.6 131.9 %layer.1 = (bf16[256,2560]{1,0:T(8,128)(2,1)}, bf16[256,2560]{1,0:T(8,128)(2,1)}, bf16[256,128]{1,0:T(8,128)(2,1)}, bf16[256,128]{1,0:T(8,128)(2,1)}, f32[40,256...) custom-call(s32[1,32]{1,0:T(1,128)} %docs_ref.1, bf16[256,2560]{1,0:T(8,128)(2,1)} %bitcast.16, ...), custom_call_target="tpu_custom_call" | custom-call | tf_op jit(solution)/shard_map/layer/pallas_call | solution.py:683
  132.5 3.4 %emit.1 = (bf16[256,2560]{1,0:T(8,128)(2,1)}, bf16[256,2560]{1,0:T(8,128)(2,1)}, bf16[256,128]{1,0:T(8,128)(2,1)}, bf16[256,128]{1,0:T(8,128)(2,1)}, f32[40,256]...) custom-call(bf16[256,2560]{1,0:T(8,128)(2,1)} %get-tuple-element.24.refs_0_, ...), custom_call_target="tpu_custom_call" | custom-call | tf_op jit(solution)/shard_map/emit/pallas_call | solution.py:718

commit v4 on v3

--- a/solution.py
+++ b/solution.py
@@ -231,6 +231,8 @@
     def gather_end(table, own, size, targets, offset):
         for k, target in enumerate(targets):
             gather_copy(table, (own + size - 1 - k) % size, target, offset + k).wait_recv()
+
+    def gather_sent(table, own, targets, offset):
         for k, target in enumerate(targets):
             gather_copy(table, own, target, offset + k).wait_send()
 
@@ -571,8 +573,8 @@
                 for d in range(2):
                     f_buf[c, d] = outside(c, d)
 
+        chains(0)
         exchanges(1)
-        chains(0)
         chains(1)
         exchanges(0)
 
@@ -628,6 +630,21 @@
         [to_row(bias_sum), to_row(decay_sum), to_row(skip_sum), jnp.zeros((5, 128), F32)], axis=0
     )
     gather_start(column_sums, column, sums, in_column, 13)
+
+    def drain(c, carry):
+        @pl.when(z < NZ - 1)
+        def _():
+            links[0](c).wait_send()
+
+        @pl.when(z > 0)
+        def _():
+            links[1](c).wait_send()
+
+        for stage in range(2, 6):
+            links[stage](c).wait_send()
+        return carry
+
+    lax.fori_loop(0, CHUNKS, drain, 0)
     gather_end(column_sums, column, 2 * NZ, in_column, 13)
     gather_start(plane_sums, cell, jnp.sum(column_sums[...], axis=0), in_plane, 28)
     gather_end(plane_sums, cell, NX * NY, in_plane, 28)
@@ -636,20 +653,11 @@
     decay_out[...] = sums[1:2, :HEADS]
     skip_out[...] = sums[2:3, :HEADS]
 
-    def drain(c, carry):
-        @pl.when(z < NZ - 1)
-        def _():
-            links[0](c).wait_send()
-
-        @pl.when(z > 0)
-        def _():
-            links[1](c).wait_send()
-
-        for stage in range(2, 6):
-            links[stage](c).wait_send()
-        return carry
-
-    lax.fori_loop(0, CHUNKS, drain, 0)
+    gather_sent(zlam, z, along_z, 0)
+    gather_sent(xlam, x, along_x, 7)
+    gather_sent(ylam, y, along_y, 10)
+    gather_sent(column_sums, column, in_column, 13)
+    gather_sent(plane_sums, cell, in_plane, 28)
 
 
 def emit_kernel(*refs):

time: 136 us -> 136 us (level)
  no operation moved by 1% of the time
where the time goes in v4:
time: 136 us
  Pallas kernels  135 us (99%)
    pallas_call x1, Pallas kernels, local(): pl.pallas_call(layer_kernel, out_shape=(shape((LEN, WIDE), BF16), shape((...  132 us
    pallas_call x1, Pallas kernels, local(): pl.pallas_call(emit_kernel, out_shape=tuple((shape(o.shape, o.dtype) for...  3.36 us

profile of v4, /device:TPU:1, one launch (start us, length us, event | category | flops | bytes accessed | tf_op | source)
XLA Modules:
  0.0 135.5 jit_solution(8076021285465811663)
XLA Ops:
  0.6 131.5 %layer.1 = (bf16[256,2560]{1,0:T(8,128)(2,1)}, bf16[256,2560]{1,0:T(8,128)(2,1)}, bf16[256,128]{1,0:T(8,128)(2,1)}, bf16[256,128]{1,0:T(8,128)(2,1)}, f32[40,256...) custom-call(s32[1,32]{1,0:T(1,128)} %docs_ref.1, bf16[256,2560]{1,0:T(8,128)(2,1)} %bitcast.16, ...), custom_call_target="tpu_custom_call" | custom-call | tf_op jit(solution)/shard_map/layer/pallas_call | solution.py:691
  132.2 3.4 %emit.1 = (bf16[256,2560]{1,0:T(8,128)(2,1)}, bf16[256,2560]{1,0:T(8,128)(2,1)}, bf16[256,128]{1,0:T(8,128)(2,1)}, bf16[256,128]{1,0:T(8,128)(2,1)}, f32[40,256]...) custom-call(bf16[256,2560]{1,0:T(8,128)(2,1)} %get-tuple-element.24.refs_0_, ...), custom_call_target="tpu_custom_call" | custom-call | tf_op jit(solution)/shard_map/emit/pallas_call | solution.py:726
